TPU v7x, 512 devices: a whole 4x4x16 slice. The times are simulated.
512 devices in a mesh: gx: 32 (over z, core), gy: 16 (over x, y).
Axes of the slice: x: 4, y: 4, z: 16, core: 2. Of those that a mesh axis runs over, the one named last changes fastest.
Arguments:
- points: bfloat16 [262144, 128], P(('gx', 'gy')), may hold values from -6 to 6
- cotangent: bfloat16 [262144, 128], P(('gx', 'gy')), may hold values from -6 to 6
- local_tiles: bfloat16 [262144, 384], P(('gx', 'gy')), may hold values from -0.25 to 0.25
- local_source: int32 [2048, 3], P(('gx', 'gy')), may hold values from 0 to 3
- halo_tiles: bfloat16 [524288, 128], P(('gx', 'gy')), may hold values from -0.25 to 0.25
- cluster_fine: int32 [262144], P(('gx', 'gy')), may hold values from 0 to 511
- cluster_mid: int32 [262144], P(('gx', 'gy')), may hold values from 0 to 511
- cluster_coarse: int32 [262144], P(('gx', 'gy')), may hold values from 0 to 63
- near_weight: bfloat16 [128, 128], replicated, may hold values from -0.5 to 0.5
- up_weights: bfloat16 [3, 128, 128], replicated, may hold values from -0.5 to 0.5
- down_weights: bfloat16 [3, 128, 128], replicated, may hold values from -0.5 to 0.5
Outputs:
- mixed: bfloat16 [262144, 128], P(('gx', 'gy'))
- point_grad: bfloat16 [262144, 128], P(('gx', 'gy'))
- weight_grads: float32 [7, 128, 128], replicated
All inputs are finite; a program needn't handle non-finite values.
Results may differ from a plain program's by a relative error of at most 0.018.
Values may be sent and summed in bfloat16 or wider, within the bound.
A program may use at most 64 MiB of HBM per device.

v0:
```python
import math

import jax
import jax.numpy as jnp
from jax import lax
from jax.sharding import PartitionSpec as P

BLK = 128
KL = 3
C0_DEV = 32


EPSILON = 1e-05


def with_halo(block, sides, width):
    for axis, dim in sides:
        count = lax.axis_size(axis)
        forward = [(i, i + 1) for i in range(count - 1)]
        backward = [(target, source) for source, target in forward]
        low = lax.ppermute(
            lax.slice_in_dim(block, block.shape[dim] - width, None, axis=dim), axis, forward
        )
        high = lax.ppermute(lax.slice_in_dim(block, 0, width, axis=dim), axis, backward)
        block = jnp.concatenate([low, block, high], axis=dim)
    return block


def one_hot(cluster, cluster_count):
    return (cluster[:, None] == jnp.arange(cluster_count, dtype=jnp.int32)[None, :]).astype(
        jnp.bfloat16
    )


def coarse_total(partial_value):
    return lax.psum(partial_value, ("gx", "gy"))


def level_total(level_index, partial_value):
    if level_index == 0:
        return lax.psum(partial_value, "gy")
    return coarse_total(partial_value)


def facing(received):
    from_x = jnp.stack([received[0, 1:3], received[3, 1:3]], axis=0)
    from_y = jnp.stack([received[1:3, 0], received[1:3, 3]], axis=1)
    return (from_x, from_y)


def on_device(
    points,
    cotangent,
    local_tiles,
    local_source,
    halo_tiles,
    cluster_fine,
    cluster_mid,
    cluster_coarse,
    near_weight,
    up_weights,
    down_weights,
):
    points_here, features = points.shape
    blocks = points_here // BLK
    tile_grid = local_tiles.reshape(blocks, BLK, KL, BLK)
    blocked = points.reshape(blocks, BLK, features)
    corners = blocked.reshape(2, 2, BLK, features)
    halo_grid = halo_tiles.reshape(2, 2, 2, BLK, BLK)
    received_points = with_halo(corners, (("gx", 0), ("gy", 1)), 1)
    from_x, from_y = facing(received_points)
    sources = blocked[local_source]
    near_field = jnp.einsum(
        "bikj,bkjc->bic", tile_grid, sources, preferred_element_type=jnp.float32
    )
    edge_term = jnp.einsum(
        "ijts,ijsc->ijtc", halo_grid[:, :, 0], from_x, preferred_element_type=jnp.float32
    )
    edge_term = edge_term + jnp.einsum(
        "ijts,ijsc->ijtc", halo_grid[:, :, 1], from_y, preferred_element_type=jnp.float32
    )
    near_field = jnp.concatenate(
        [near_field + edge_term.reshape(4, BLK, features), near_field[4:]], axis=0
    )
    near_values = near_field.reshape(points_here, features).astype(jnp.bfloat16)
    size_x = lax.axis_size("gx")
    size_y = lax.axis_size("gy")
    cluster_counts = [C0_DEV * size_y, size_x * size_y, size_x * size_y // 8]
    clusters = [cluster_fine, cluster_mid, cluster_coarse]
    selectors = []
    inputs_list = []
    normed_list = []
    inverse_list = []
    gathered_list = []
    level_input = points
    for level_index in range(3):
        selector = one_hot(clusters[level_index], cluster_counts[level_index])
        up_values = jnp.dot(
            level_input, up_weights[level_index], preferred_element_type=jnp.float32
        ).astype(jnp.bfloat16)
        partial_value = jnp.einsum(
            "pk,pc->kc", selector, up_values, preferred_element_type=jnp.float32
        )
        summed = level_total(level_index, partial_value)
        inverse_rms = lax.rsqrt(jnp.mean(summed * summed, axis=-1, keepdims=True) + EPSILON)
        normed = summed * inverse_rms
        gathered = normed[clusters[level_index]].astype(jnp.bfloat16)
        selectors.append(selector)
        inputs_list.append(level_input)
        normed_list.append(normed)
        inverse_list.append(inverse_rms)
        gathered_list.append(gathered)
        level_input = gathered
    combined = points.astype(jnp.float32) + jnp.dot(
        near_values, near_weight, preferred_element_type=jnp.float32
    )
    for level_index in range(3):
        combined = combined + jnp.dot(
            gathered_list[level_index],
            down_weights[level_index],
            preferred_element_type=jnp.float32,
        )
    mixed = combined.astype(jnp.bfloat16)
    near_grad = jnp.dot(cotangent, near_weight.T, preferred_element_type=jnp.float32).astype(
        jnp.bfloat16
    )
    up_grads = [None] * 3
    down_grads = [None] * 3
    upper = None
    for level_index in (2, 1, 0):
        level_grad = jnp.dot(
            cotangent, down_weights[level_index].T, preferred_element_type=jnp.float32
        )
        if upper is not None:
            level_grad = level_grad + jnp.dot(
                upper, up_weights[level_index + 1].T, preferred_element_type=jnp.float32
            )
        level_grad = level_grad.astype(jnp.bfloat16)
        partial_value = jnp.einsum(
            "pk,pc->kc", selectors[level_index], level_grad, preferred_element_type=jnp.float32
        )
        summed_grad = level_total(level_index, partial_value)
        normed = normed_list[level_index]
        summed_grad = inverse_list[level_index] * (
            summed_grad - normed * jnp.mean(summed_grad * normed, axis=-1, keepdims=True)
        )
        upper = summed_grad[clusters[level_index]].astype(jnp.bfloat16)
        up_grads[level_index] = jnp.dot(
            inputs_list[level_index].T, upper, preferred_element_type=jnp.float32
        )
        down_grads[level_index] = jnp.dot(
            gathered_list[level_index].T, cotangent, preferred_element_type=jnp.float32
        )
    blocked_grad = near_grad.reshape(blocks, BLK, features)
    pieces = jnp.einsum(
        "bikj,bic->bkjc", tile_grid, blocked_grad, preferred_element_type=jnp.float32
    )
    source_table = (
        local_source.reshape(-1)[:, None] == jnp.arange(blocks, dtype=jnp.int32)[None, :]
    ).astype(jnp.float32)
    returned = jnp.einsum(
        "mb,mjc->bjc",
        source_table,
        pieces.reshape(blocks * KL, BLK, features),
        precision=lax.Precision.HIGHEST,
    )
    corner_grad = blocked_grad.reshape(2, 2, BLK, features)
    push_x = jnp.einsum(
        "ijts,ijtc->ijsc", halo_grid[:, :, 0], corner_grad, preferred_element_type=jnp.float32
    )
    push_y = jnp.einsum(
        "ijts,ijtc->ijsc", halo_grid[:, :, 1], corner_grad, preferred_element_type=jnp.float32
    )
    outgoing = jnp.stack([push_x, push_y], axis=2)
    incoming = with_halo(outgoing.astype(jnp.bfloat16), (("gx", 0), ("gy", 1)), 1).astype(
        outgoing.dtype
    )
    back_x = jnp.stack([incoming[0, 1:3, 0], incoming[3, 1:3, 0]], axis=0)
    back_y = jnp.stack([incoming[1:3, 0, 1], incoming[1:3, 3, 1]], axis=1)
    edge_back = back_x + back_y
    returned = jnp.concatenate(
        [returned + edge_back.reshape(4, BLK, features), returned[4:]], axis=0
    )
    point_grad = (
        cotangent.astype(jnp.float32)
        + returned.reshape(points_here, features)
        + jnp.dot(upper, up_weights[0].T, preferred_element_type=jnp.float32)
    ).astype(jnp.bfloat16)
    grad_list = (
        [jnp.dot(near_values.T, cotangent, preferred_element_type=jnp.float32)]
        + up_grads
        + down_grads
    )
    grad_total = lax.psum(jnp.stack(grad_list), ("gx", "gy"))
    weight_grads = grad_total * (1.0 / math.sqrt(points_here * size_x * size_y))
    return (mixed, point_grad, weight_grads)


def solution(mesh):
    in_specs = (
        P(("gx", "gy"), None),
        P(("gx", "gy"), None),
        P(("gx", "gy"), None),
        P(("gx", "gy"), None),
        P(("gx", "gy"), None),
        P(("gx", "gy")),
        P(("gx", "gy")),
        P(("gx", "gy")),
        P(),
        P(),
        P(),
    )
    out_specs = (P(("gx", "gy"), None), P(("gx", "gy"), None), P())
    return jax.shard_map(
        on_device, mesh=mesh, in_specs=in_specs, out_specs=out_specs, check_vma=False
    )
```

profile of v0, /device:TPU:2, one launch (start us, length us, event | category | flops | bytes accessed | tf_op | source)
XLA Modules:
  0.0 2080.8 jit_solution(11196091404114034025)
XLA Ops:
  7.2 2.2 fusion.4
  9.5 0.8 copy-done.2
  11.0 1.7 collective-permute-start
  12.7 1.3 collective-permute-start.1
  14.7 0.7 fusion.27
  15.4 4.9 collective-permute-start.4
  20.3 1.3 collective-permute-start.5
  22.2 0.9 fusion.11
  23.2 0.9 fusion.54
  24.1 0.9 fusion.61
  24.9 0.7 eq.63
  25.6 0.7 copy-done.27
  29.9 0.9 pad_maximum_fusion.1
  30.8 3.5 collective-permute-start.2
  34.3 4.5 collective-permute-start.3
  38.9 0.8 fusion.90
  39.7 2.0 collective-permute-start.6
  41.7 6.0 collective-permute-start.7
  49.2 0.9 fusion.18
  50.2 80.1 %all-reduce.8.cloned.1.call-done = f32[512,128]{1,0:T(8,128)} async-done(((f32[512,128]{1,0:T(8,128)}), f32[512,128]{1,0:T(8,128)}) %all-reduce.8.cloned.1.call-update) | async-done | bytes 262160 | tf_op jit(solution)/shard_map/psum | solution.py:41
  130.3 1.2 multiply_reduce_fusion.3
  131.6 1.1 gather_fusion.1
  132.7 1.2 fusion.5
  134.0 0.9 convolution_add_fusion.7
  134.9 458.4 %all-reduce.10.cloned.1.call-done = f32[512,128]{1,0:T(8,128)} async-done(((f32[512,128]{1,0:T(8,128)}), f32[512,128]{1,0:T(8,128)}) %all-reduce.10.cloned.1.call-update) | async-done | bytes 262160 | tf_op jit(solution)/shard_map/psum | solution.py:36
  593.3 1.2 multiply_reduce_fusion.2
  595.2 1.0 gather_fusion.2
  596.2 0.9 fusion.10
  597.3 0.9 convolution_add_fusion.6
  598.1 0.9 convert_bitcast_fusion
  599.3 436.6 %all-reduce.18.cloned.1.call-done = (f32[64,128]{1,0:T(8,128)}, f32[64,128]{1,0:T(8,128)}) async-done(((f32[64,128]{1,0:T(8,128)}, f32[64,128]{1,0:T(8,128)}), (f32[64,128]{1,0:T(8,128)}, f32[64,128]{1,0:T(8,128)})) %all-reduce.18.cloned.1.call-update) | async-done | bytes 65552 | tf_op jit(solution)/shard_map/psum | solution.py:36
  1035.9 0.9 multiply_reduce_fusion.5
  1036.9 1.0 multiply_reduce_fusion.4
  1038.1 1.3 gather_fusion.4
  1039.4 1.3 fusion.7
  1041.9 448.9 %all-reduce.12.cloned.1.call-done = f32[512,128]{1,0:T(8,128)} async-done(((f32[512,128]{1,0:T(8,128)}), f32[512,128]{1,0:T(8,128)}) %all-reduce.12.cloned.1.call-update) | async-done | bytes 262160 | tf_op jit(solution)/shard_map/psum | solution.py:36
  1490.8 1.3 multiply_reduce_fusion.1
  1492.8 1.3 gather_fusion.5
  1494.1 1.2 fusion.6
  1495.5 1.1 gather_fusion.3
  1496.5 0.8 fusion
  1497.4 108.5 %all-reduce.14.cloned.1.call-done = f32[512,128]{1,0:T(8,128)} async-done(((f32[512,128]{1,0:T(8,128)}), f32[512,128]{1,0:T(8,128)}) %all-reduce.14.cloned.1.call-update) | async-done | bytes 262160 | tf_op jit(solution)/shard_map/psum | solution.py:41
  1605.9 1.3 multiply_reduce_fusion
  1607.4 1.3 gather_fusion.6
  1610.2 0.8 copy-done.14
  1611.0 0.8 fusion.3
  1611.8 460.3 %all-reduce.16.cloned.1.call-done = f32[7,128,128]{2,1,0:T(8,128)} async-done(((f32[7,128,128]{2,1,0:T(8,128)}), f32[7,128,128]{2,1,0:T(8,128)}) %all-reduce.16.cloned.1.call-update) | async-done | bytes 458768 | tf_op jit(solution)/shard_map/psum | solution.py:194
  2072.1 1.8 broadcast_multiply_fusion
  (137 shorter events, 12.0 us)
Async XLA Ops:
  7.2 6.8 copy-start
  7.2 123.1 %all-reduce.8.cloned.1.call-start = ((), (), s32[]{:S(2)}) async-start(), calls=%async_computation | async-start | bytes 524288 | tf_op jit(solution)/shard_map/psum | solution.py:41
  9.4 0.9 copy-start.2
  9.4 4.6 copy-start.1
  9.4 4.8 copy-start.5
  9.5 583.8 %all-reduce.10.cloned.1.call-start = ((), (), s32[]{:S(2)}) async-start(), calls=%async_computation.1 | async-start | bytes 524288 | tf_op jit(solution)/shard_map/psum | solution.py:36
  11.0 17.6 collective-permute-start
  12.7 15.9 collective-permute-start.1
  14.7 7.5 copy-start.16
  15.4 6.2 copy-start.29
  15.4 23.3 %collective-permute-start.4 = (bf16[1,2,2,128,128]{4,3,1,0,2:T(8,128)(2,1)}, bf16[1,2,2,128,128]{4,3,1,0,2:T(8,128)(2,1)S(1)}, u32[]{:S(2)}, u32[]{:S(2)}) collective-permute-start(bf16[1,2,2,128,128]{4,3,1,0,2:T(8,128)(2,1)} %get-tuple-element.13), channel_id=1, source_target_pairs={{0,16},{16,32},{32,48},{48,64},{64,80},{80,96},{96,112},{112,128},... | collective-permute-start | bytes 393224 | tf_op jit(solution)/shard_map/ppermute | solution.py:21
  20.3 1.3 copy-start.34
  20.3 18.5 collective-permute-start.5
  23.2 3.7 copy-start.15
  24.1 0.9 copy-start.32
  25.6 0.7 copy-start.27
  27.9 0.7 copy-start.31
  30.8 17.0 collective-permute-start.2
  34.3 13.5 collective-permute-start.3
  39.7 8.1 copy-start.6
  39.7 558.4 %collective-permute-start.6 = (bf16[4,1,2,128,128]{4,3,1,0,2:T(8,128)(2,1)}, bf16[4,1,2,128,128]{4,3,1,0,2:T(8,128)(2,1)S(1)}, u32[]{:S(2)}, u32[]{:S(2)}) collective-permute-start(bf16[4,1,2,128,128]{4,3,1,0,2:T(8,128)(2,1)} %get-tuple-element.11), channel_id=1, source_target_pairs={{0,1},{1,2},{2,3},{3,4},{4,5},{5,6},{6,7},{7,8},{8,9},{9,10},{10,1... | collective-permute-start | bytes 786440 | tf_op jit(solution)/shard_map/ppermute | solution.py:21
  41.7 556.4 %collective-permute-start.7 = (bf16[4,1,2,128,128]{4,3,1,0,2:T(8,128)(2,1)}, bf16[4,1,2,128,128]{4,3,1,0,2:T(8,128)(2,1)}, u32[]{:S(2)}, u32[]{:S(2)}) collective-permute-start(bf16[4,1,2,128,128]{4,3,1,0,2:T(8,128)(2,1)} %get-tuple-element.12), channel_id=1, source_target_pairs={{1,0},{2,1},{3,2},{4,3},{5,4},{6,5},{7,6},{8,7},{9,8},{10,9},{11,1... | collective-permute-start | bytes 786440 | tf_op jit(solution)/shard_map/ppermute | solution.py:24
  47.8 0.8 copy-start.18
  47.9 0.9 copy-start.20
  130.3 1.2 copy-start.3
  131.6 1.1 copy-start.23
  133.9 902.0 %all-reduce.18.cloned.1.call-start = ((), (), s32[]{:S(2)}) async-start(), calls=%async_computation.5 | async-start | bytes 131072 | tf_op jit(solution)/shard_map/psum | solution.py:36
  593.3 1.2 copy-start.4
  594.5 0.7 copy-start.25
  595.1 1.1 copy-start.35
  596.2 1.0 copy-start.8
  597.2 893.6 %all-reduce.12.cloned.1.call-start = ((), (), s32[]{:S(2)}) async-start(), calls=%async_computation.2 | async-start | bytes 524288 | tf_op jit(solution)/shard_map/psum | solution.py:36
  1035.9 1.0 copy-start.21
  1036.9 1.0 copy-start.22
  1038.0 1.4 copy-start.12
  1038.0 1.4 copy-start.24
  1038.0 1.4 copy-start.28
  1040.7 0.7 copy-start.33
  1040.7 565.2 %all-reduce.14.cloned.1.call-start = ((), (), s32[]{:S(2)}) async-start(), calls=%async_computation.3 | async-start | bytes 524288 | tf_op jit(solution)/shard_map/psum | solution.py:41
  1490.8 1.3 copy-start.10
  1492.1 0.7 copy-start.26
  1492.7 1.3 copy-start.11
  1492.7 1.4 copy-start.30
  1495.4 576.7 %all-reduce.16.cloned.1.call-start = ((), (), s32[]{:S(2)}) async-start(), calls=%async_computation.4 | async-start | bytes 917504 | tf_op jit(solution)/shard_map/psum | solution.py:194
  1495.5 1.1 copy-start.7
  1605.9 1.3 copy-start.9
  1607.4 1.4 copy-start.13
  1610.2 0.8 copy-start.14
  (2 other events, 1.2 us)
Sparse Core Ops, SparseCore 0:
  11.2 119.0 all-reduce.7
  136.6 456.6 all-reduce.9
  599.5 436.4 all-reduce.17
  1042.1 448.6 all-reduce.11
  1495.5 110.3 all-reduce.13
  1612.7 459.3 all-reduce.15
where the time goes:
time: 2080 us
  waiting for transfers between devices  1990 us (96%)
  starting transfers between devices  25.4 us (1%)
    psum x3, waiting for transfers between devices, coarse_total(): return lax.psum(partial_value, ('gx', 'gy'))  1340 us
    psum x1, waiting for transfers between devices, on_device(): grad_total = lax.psum(jnp.stack(grad_list), ('gx', 'gy'))  460 us
    psum x2, waiting for transfers between devices, level_total(): return lax.psum(partial_value, 'gy')  189 us
  transfers between devices with their start and end apart: 14, of which 6 were waited for; matrix products, arithmetic and copies ran while one was open for 1% of the time, Pallas kernels for 0%

commit v1 on v0

v1 whole, which is shorter than its diff:
```python
import functools
import math

import jax
import jax.numpy as jnp
from jax import lax
from jax.experimental import pallas as pl
from jax.experimental.pallas import tpu as pltpu
from jax.sharding import PartitionSpec as P

BLK = 128
C = 128
PTS = 512
OWN0 = 32
EPSILON = 1e-05
MESH = pl.DeviceIdType.MESH
F32, BF16 = jnp.float32, jnp.bfloat16

NN = ((1,), (0,))
NT = ((1,), (1,))
TN = ((0,), (0,))


def dot(a, b, dims=NN):
    return lax.dot_general(a, b, (dims, ((), ())), preferred_element_type=F32)


def dot_split(a, b, dims=NN):
    high = a.astype(BF16)
    low = (a - high.astype(F32)).astype(BF16)
    return dot(high, b, dims) + dot(low, b, dims)


def one_hot_rows(ids, first, count):
    rows = lax.broadcasted_iota(jnp.int32, (count, ids.shape[1]), 0) + first
    return jnp.where(rows == ids, 1.0, 0.0).astype(BF16)


def inverse_rms(summed):
    return lax.rsqrt(jnp.mean(summed * summed, axis=-1, keepdims=True) + EPSILON)


def norm_back(raw, normed, inverse):
    return inverse * (raw - normed * jnp.mean(raw * normed, axis=-1, keepdims=True))


def kernel(
    size_x,
    size_y,
    pts_ref,
    cot_ref,
    tiles_ref,
    src_ref,
    halo_ref,
    c0_ref,
    c1_ref,
    c2_ref,
    nw_ref,
    up_ref,
    dn_ref,
    mixed_ref,
    pg_ref,
    wg_ref,
    ot0,
    ot1,
    ot2,
    near,
    ret,
    nv,
    spx,
    spy,
    fx,
    fy,
    bx,
    by,
    ids,
    s_u0,
    r_u0,
    s_t0,
    r_t0,
    s_p1,
    r_p1,
    z_p1,
    p1,
    s_u1,
    r_u1,
    z_u1,
    u1,
    n0all,
    sg0all,
    s_p2,
    r_p2,
    z_p2,
    g_p2,
    s_d,
    r_d,
    z_d,
    g_d,
    send_sem,
    recv_sem,
    halo_send,
    halo_recv,
):
    size_z = size_x // 2
    size_q = 2 * size_y
    k1 = size_x * size_y
    k2 = k1 // 8
    a = lax.axis_index("gx")
    b = lax.axis_index("gy")
    z = lax.div(a, 2)
    core = lax.rem(a, 2)
    q = core * size_y + b
    scale = 1.0 / math.sqrt(PTS * size_x * size_y)

    def peer(kind, o):
        if kind == "y":
            i = lax.rem(b + o, size_y)
            return i, (a, i)
        if kind == "z":
            i = lax.rem(z + o, size_z)
            return i, (i * 2 + core, b)
        i = lax.rem(q + o, size_q)
        return i, (z * 2 + lax.div(i, size_y), lax.rem(i, size_y))

    count = {"y": size_y, "z": size_z, "q": size_q}

    def exchange(kind, step, source, target):
        def body(o, carry):
            i, device = peer(kind, o)
            pltpu.make_async_remote_copy(
                src_ref=source(i),
                dst_ref=target,
                send_sem=send_sem.at[step],
                recv_sem=recv_sem.at[step],
                device_id=device,
                device_id_type=MESH,
            ).start()
            return carry

        lax.fori_loop(1, count[kind], body, 0)

    def arrived(step, ref):
        pltpu.make_async_copy(ref, ref, recv_sem.at[step]).wait()

    def sent(step, ref):
        pltpu.make_async_copy(ref, ref, send_sem.at[step]).wait()

    barrier = pltpu.get_barrier_semaphore()

    def greet(kind):
        def body(o, carry):
            _, device = peer(kind, o)
            pl.semaphore_signal(barrier, inc=1, device_id=device, device_id_type=MESH)
            return carry

        lax.fori_loop(1, count[kind], body, 0)

    greet("z")
    greet("q")
    beside = lax.rem(a + size_x - 1 + 2 * core, size_x)
    pl.semaphore_signal(barrier, inc=1, device_id=(beside, b), device_id_type=MESH)

    points = pts_ref[...].reshape(PTS, C)
    cot = cot_ref[...]
    c0, c1, c2 = c0_ref[...], c1_ref[...], c2_ref[...]
    ot0[...] = one_hot_rows(c0, 0, OWN0 * size_y)
    ot1[...] = one_hot_rows(c1, 0, k1)
    ot2[...] = one_hot_rows(c2, 0, C)
    both = dot(ot0[...], jnp.concatenate([points, cot], axis=1))
    s_u0[...] = both[:, :C].astype(BF16)
    s_t0[...] = both[:, C:].astype(BF16)
    ids[b] = c0 * 1024 + c1
    lane = lax.broadcasted_iota(jnp.int32, (k2, C), 1)
    t2 = dot(ot2[...], cot)[:k2]
    s_p1[:, :C] = dot(ot1[...], cot).astype(BF16)
    counts = dot(ot1[...], ot2[...], NT)
    s_p1[2 * k2 :, C:] = counts[2 * k2 :].astype(BF16)
    s_p1[:k2, C:] = jnp.where(lane < k2, counts[:k2], pltpu.roll(t2, C - k2, 1)).astype(BF16)
    s_p1[k2 : 2 * k2, C:] = jnp.where(lane < k2, counts[k2 : 2 * k2], t2).astype(BF16)

    near_grad = dot(cot, nw_ref[...], NT).astype(BF16)
    returned = [jnp.zeros((BLK, C), F32)] * 4
    for t in range(4):
        rows = slice(t * BLK, (t + 1) * BLK)
        tile = tiles_ref[rows, :]
        sources = jnp.concatenate([pts_ref[src_ref[t, k]] for k in range(3)], axis=0)
        near[t] = dot(tile, sources)
        grad = near_grad[rows]
        pieces = dot(tile, grad, TN)
        for k in range(3):
            piece = pieces[k * BLK : (k + 1) * BLK]
            for s in range(4):
                returned[s] = returned[s] + jnp.where(src_ref[t, k] == s, piece, 0.0)
        spx[t] = dot(halo_ref[2 * t], grad, TN).astype(BF16)
        spy[t] = dot(halo_ref[2 * t + 1], grad, TN).astype(BF16)
    for s in range(4):
        ret[s] = returned[s]

    pl.semaphore_wait(barrier, size_z - 1 + size_q - 1 + 1)

    exchange("y", 0, lambda i: ids.at[b], ids.at[b])
    exchange("y", 1, lambda i: s_u0.at[pl.ds(i * OWN0, OWN0)], r_u0.at[b])
    exchange("q", 2, lambda i: s_p1.at[pl.ds(i * 16, 16)], r_p1.at[q])
    exchange("y", 3, lambda i: s_t0.at[pl.ds(i * OWN0, OWN0)], r_t0.at[b])
    has = (a > 0, a < size_x - 1, b > 0, b < size_y - 1)

    def halo_copies(side):
        if side == 0:
            return [[(pts_ref.at[pl.ds(0, 2)], fx.at[pl.ds(2, 2)])], [(spx.at[pl.ds(0, 2)], bx.at[pl.ds(2, 2)])]]
        if side == 1:
            return [[(pts_ref.at[pl.ds(2, 2)], fx.at[pl.ds(0, 2)])], [(spx.at[pl.ds(2, 2)], bx.at[pl.ds(0, 2)])]]
        if side == 2:
            return [[(pts_ref.at[i], fy.at[i + 1]) for i in (0, 2)], [(spy.at[i], by.at[i + 1]) for i in (0, 2)]]
        return [[(pts_ref.at[i], fy.at[i - 1]) for i in (1, 3)], [(spy.at[i], by.at[i - 1]) for i in (1, 3)]]

    neighbour = ((a - 1, b), (a + 1, b), (a, b - 1), (a, b + 1))
    for side in range(4):

        @pl.when(has[side])
        def _(side=side):
            for kind in range(2):
                for source, target in halo_copies(side)[kind]:
                    pltpu.make_async_remote_copy(
                        src_ref=source,
                        dst_ref=target,
                        send_sem=halo_send.at[2 * side + kind],
                        recv_sem=halo_recv.at[2 * (side ^ 1) + kind],
                        device_id=neighbour[side],
                        device_id_type=MESH,
                    ).start()

    arrived(0, ids.at[pl.ds(0, size_y - 1)])
    pair_counts = jnp.zeros((OWN0, k1), F32)
    for i in range(size_y):
        packed = ids[i]
        fine = lax.shift_right_logical(packed, 10)
        mid = lax.bitwise_and(packed, 1023)
        pair_counts = pair_counts + dot(
            one_hot_rows(fine, b * OWN0, OWN0), one_hot_rows(mid, 0, k1), NT
        )
    pair_counts = pair_counts.astype(BF16)

    r_u0[b] = s_u0[pl.ds(pl.multiple_of(b * OWN0, OWN0), OWN0), :]
    arrived(1, r_u0.at[pl.ds(0, size_y - 1)])
    u0 = jnp.sum(r_u0[...].astype(F32), axis=0)
    summed0 = dot_split(u0, up_ref[0])
    inverse0 = inverse_rms(summed0)
    normed0 = summed0 * inverse0
    n0 = normed0.astype(BF16)
    s_u1[...] = dot(pair_counts, n0, TN).astype(BF16)
    exchange("q", 4, lambda i: s_u1.at[pl.ds(i * 16, 16)], r_u1.at[q])
    mine32 = pl.ds(pl.multiple_of(b * OWN0, OWN0), OWN0)
    n0all[mine32, :] = n0
    exchange("y", 5, lambda i: n0all.at[mine32], n0all.at[mine32])

    mine16 = pl.ds(pl.multiple_of(q * 16, 16), 16)
    r_p1[q] = s_p1[mine16, :]
    arrived(2, r_p1.at[pl.ds(0, size_q - 1)])
    z_p1[z] = jnp.sum(r_p1[...].astype(F32), axis=0).astype(BF16)
    exchange("z", 6, lambda i: z_p1.at[z], z_p1.at[z])

    r_t0[b] = s_t0[mine32, :]
    arrived(3, r_t0.at[pl.ds(0, size_y - 1)])
    t0 = jnp.sum(r_t0[...].astype(F32), axis=0)

    for side in range(4):
        got = (
            (fx.at[pl.ds(0, 2)], bx.at[pl.ds(0, 2)])
            if side == 0
            else (fx.at[pl.ds(2, 2)], bx.at[pl.ds(2, 2)])
            if side == 1
            else (fy.at[pl.ds(0, 2)], by.at[pl.ds(0, 2)])
        )

        @pl.when(has[side])
        def _(side=side, got=got):
            for kind in range(2):
                pltpu.make_async_copy(got[kind], got[kind], halo_recv.at[2 * side + kind]).wait()

        @pl.when(jnp.logical_not(has[side]))
        def _(side=side):
            for i in ((0, 1), (2, 3), (0, 2), (1, 3))[side]:
                for ref in ((fx, bx) if side < 2 else (fy, by)):
                    ref[i] = jnp.zeros((BLK, C), BF16)

    for t in range(4):
        total = near[t] + dot(halo_ref[2 * t], fx[t]) + dot(halo_ref[2 * t + 1], fy[t])
        nv[pl.ds(t * BLK, BLK), :] = total.astype(BF16)
        ret[t] = ret[t] + bx[t].astype(F32) + by[t].astype(F32)
    near_part = dot(nv[...], cot, TN)
    down0_part = dot(n0, t0.astype(BF16), TN)
    s_p2[...] = jnp.concatenate(
        [near_part.reshape(size_y, 8, C), down0_part.reshape(size_y, 8, C)], axis=1
    ).astype(BF16)
    exchange("q", 7, lambda i: s_p2.at[lax.rem(i, size_y)], r_p2.at[q])

    r_u1[q] = s_u1[mine16, :]
    arrived(4, r_u1.at[pl.ds(0, size_q - 1)])
    z_u1[z] = jnp.sum(r_u1[...].astype(F32), axis=0).astype(BF16)
    exchange("z", 8, lambda i: z_u1.at[z], z_u1.at[z])

    arrived(6, z_p1.at[pl.ds(0, size_z - 1)])
    p1[mine16, :] = jnp.sum(z_p1[...].astype(F32), axis=0).astype(BF16)
    exchange("q", 9, lambda i: p1.at[mine16], p1.at[mine16])

    r_p2[q] = s_p2[b]
    arrived(7, r_p2.at[pl.ds(0, size_q - 1)])
    z_p2[z] = jnp.sum(r_p2[...].astype(F32), axis=0).astype(BF16)
    exchange("z", 10, lambda i: z_p2.at[z], z_p2.at[z])

    arrived(8, z_u1.at[pl.ds(0, size_z - 1)])
    u1[mine16, :] = jnp.sum(z_u1[...].astype(F32), axis=0).astype(BF16)
    exchange("q", 11, lambda i: u1.at[mine16], u1.at[mine16])

    arrived(10, z_p2.at[pl.ds(0, size_z - 1)])
    g_p2[b] = jnp.sum(z_p2[...].astype(F32), axis=0) * scale
    exchange("y", 12, lambda i: g_p2.at[b], g_p2.at[b])

    arrived(9, p1.at[pl.ds(0, (size_q - 1) * 16)])
    t1 = p1[:, :C]
    upper_part = p1[:k2, C:].astype(F32)
    t2 = jnp.where(lane < k2, pltpu.roll(upper_part, C - k2, 1), p1[k2 : 2 * k2, C:].astype(F32))
    t2 = t2.astype(BF16)
    counts = p1[:, C:][:, :k2]

    raw2 = dot(t2, dn_ref[2], NT)
    raw1 = dot(t1, dn_ref[1], NT)
    raw0 = dot_split(t0, dn_ref[0], NT)
    arrived(11, u1.at[pl.ds(0, (size_q - 1) * 16)])
    summed1 = dot(u1[...], up_ref[1])
    inverse1 = inverse_rms(summed1)
    normed1 = summed1 * inverse1
    n1 = normed1.astype(BF16)
    u2 = dot(counts, n1, TN)
    summed2 = dot_split(u2, up_ref[2])
    inverse2 = inverse_rms(summed2)
    normed2 = summed2 * inverse2
    n2 = normed2.astype(BF16)
    sg2 = norm_back(raw2, normed2, inverse2).astype(BF16)
    raw1 = raw1 + dot_split(dot(counts, sg2), up_ref[2], NT)
    sg1 = norm_back(raw1, normed1, inverse1).astype(BF16)
    raw0 = raw0 + dot_split(dot(pair_counts, sg1), up_ref[1], NT)
    sg0 = norm_back(raw0, normed0, inverse0).astype(BF16)
    s_d[...] = dot_split(u0, sg0, TN).reshape(size_y, 8, C)
    exchange("q", 13, lambda i: s_d.at[lax.rem(i, size_y)], r_d.at[q])
    sg0all[mine32, :] = sg0
    exchange("y", 14, lambda i: sg0all.at[mine32], sg0all.at[mine32])

    wg_ref[2] = dot(u1[...], sg1, TN) * scale
    wg_ref[3] = dot_split(u2, sg2, TN) * scale
    wg_ref[5] = dot(n1, t1, TN) * scale
    wg_ref[6] = dot(n2, t2, TN) * scale

    arrived(5, n0all.at[pl.ds(0, (size_y - 1) * OWN0)])
    combined = points.astype(F32) + dot(nv[...], nw_ref[...])
    combined = combined + dot(dot(ot0[...], n0all[...], TN).astype(BF16), dn_ref[0])
    combined = combined + dot(dot(ot1[...], n1, TN).astype(BF16), dn_ref[1])
    combined = combined + dot(dot(ot2[:k2, :], n2, TN).astype(BF16), dn_ref[2])
    mixed_ref[...] = combined.astype(BF16)

    r_d[q] = s_d[b]
    arrived(13, r_d.at[pl.ds(0, size_q - 1)])
    z_d[z] = jnp.sum(r_d[...], axis=0)
    exchange("z", 15, lambda i: z_d.at[z], z_d.at[z])

    arrived(14, sg0all.at[pl.ds(0, (size_y - 1) * OWN0)])
    upper0 = dot(ot0[...], sg0all[...], TN).astype(BF16)
    grad = cot.astype(F32) + ret[...].reshape(PTS, C) + dot(upper0, up_ref[0], NT)
    pg_ref[...] = grad.astype(BF16)

    arrived(12, g_p2.at[pl.ds(0, size_y - 1)])
    wg_ref[0] = g_p2[:, :8, :].reshape(C, C)
    wg_ref[4] = g_p2[:, 8:, :].reshape(C, C)

    arrived(15, z_d.at[pl.ds(0, size_z - 1)])
    g_d[b] = jnp.sum(z_d[...], axis=0) * scale
    exchange("y", 16, lambda i: g_d.at[b], g_d.at[b])
    for step, ref in (
        (0, ids.at[pl.ds(0, size_y - 1)]),
        (1, r_u0.at[pl.ds(0, size_y - 1)]),
        (2, r_p1.at[pl.ds(0, size_q - 1)]),
        (3, r_t0.at[pl.ds(0, size_y - 1)]),
        (4, r_u1.at[pl.ds(0, size_q - 1)]),
        (5, n0all.at[pl.ds(0, (size_y - 1) * OWN0)]),
        (6, z_p1.at[pl.ds(0, size_z - 1)]),
        (7, r_p2.at[pl.ds(0, size_q - 1)]),
        (8, z_u1.at[pl.ds(0, size_z - 1)]),
        (9, p1.at[pl.ds(0, (size_q - 1) * 16)]),
        (10, z_p2.at[pl.ds(0, size_z - 1)]),
        (11, u1.at[pl.ds(0, (size_q - 1) * 16)]),
        (12, g_p2.at[pl.ds(0, size_y - 1)]),
        (13, r_d.at[pl.ds(0, size_q - 1)]),
        (14, sg0all.at[pl.ds(0, (size_y - 1) * OWN0)]),
        (15, z_d.at[pl.ds(0, size_z - 1)]),
    ):
        sent(step, ref)
    for side in range(4):

        @pl.when(has[side])
        def _(side=side):
            for kind in range(2):
                two = fx.at[pl.ds(0, 2)]
                pltpu.make_async_copy(two, two, halo_send.at[2 * side + kind]).wait()

    arrived(16, g_d.at[pl.ds(0, size_y - 1)])
    sent(16, g_d.at[pl.ds(0, size_y - 1)])
    wg_ref[1] = g_d[...].reshape(C, C)


def on_device(
    size_x,
    size_y,
    points,
    cotangent,
    local_tiles,
    local_source,
    halo_tiles,
    cluster_fine,
    cluster_mid,
    cluster_coarse,
    near_weight,
    up_weights,
    down_weights,
):
    size_z, size_q, k1 = size_x // 2, 2 * size_y, size_x * size_y
    vmem = pl.BlockSpec(memory_space=pltpu.VMEM)
    smem = pl.BlockSpec(memory_space=pltpu.SMEM)
    k0 = OWN0 * size_y
    blocks = pltpu.VMEM((4, BLK, C), BF16)
    scratch = [
        pltpu.VMEM((k0, PTS), BF16),
        pltpu.VMEM((k1, PTS), BF16),
        pltpu.VMEM((C, PTS), BF16),
        pltpu.VMEM((4, BLK, C), F32),
        pltpu.VMEM((4, BLK, C), F32),
        pltpu.VMEM((PTS, C), BF16),
        blocks,
        blocks,
        blocks,
        blocks,
        blocks,
        blocks,
        pltpu.VMEM((size_y, 1, PTS), jnp.int32),
        pltpu.VMEM((k0, C), BF16),
        pltpu.VMEM((size_y, OWN0, C), BF16),
        pltpu.VMEM((k0, C), BF16),
        pltpu.VMEM((size_y, OWN0, C), BF16),
        pltpu.VMEM((k1, 2 * C), BF16),
        pltpu.VMEM((size_q, 16, 2 * C), BF16),
        pltpu.VMEM((size_z, 16, 2 * C), BF16),
        pltpu.VMEM((k1, 2 * C), BF16),
        pltpu.VMEM((k1, C), BF16),
        pltpu.VMEM((size_q, 16, C), BF16),
        pltpu.VMEM((size_z, 16, C), BF16),
        pltpu.VMEM((k1, C), BF16),
        pltpu.VMEM((k0, C), BF16),
        pltpu.VMEM((k0, C), BF16),
        pltpu.VMEM((size_y, 16, C), BF16),
        pltpu.VMEM((size_q, 16, C), BF16),
        pltpu.VMEM((size_z, 16, C), BF16),
        pltpu.VMEM((size_y, 16, C), F32),
        pltpu.VMEM((size_y, 8, C), F32),
        pltpu.VMEM((size_q, 8, C), F32),
        pltpu.VMEM((size_z, 8, C), F32),
        pltpu.VMEM((size_y, 8, C), F32),
        pltpu.SemaphoreType.DMA((17,)),
        pltpu.SemaphoreType.DMA((17,)),
        pltpu.SemaphoreType.DMA((8,)),
        pltpu.SemaphoreType.DMA((8,)),
    ]
    return pl.pallas_call(
        functools.partial(kernel, size_x, size_y),
        out_shape=(
            jax.ShapeDtypeStruct((PTS, C), BF16),
            jax.ShapeDtypeStruct((PTS, C), BF16),
            jax.ShapeDtypeStruct((7, C, C), F32),
        ),
        in_specs=[vmem, vmem, vmem, smem, vmem, vmem, vmem, vmem, vmem, vmem, vmem],
        out_specs=(vmem, vmem, vmem),
        scratch_shapes=scratch,
        name="layer",
        compiler_params=pltpu.CompilerParams(
            collective_id=0, has_side_effects=True, vmem_limit_bytes=48 * 1024 * 1024
        ),
    )(
        points.reshape(4, BLK, C),
        cotangent,
        local_tiles,
        local_source,
        halo_tiles.reshape(8, BLK, BLK),
        cluster_fine.reshape(1, PTS),
        cluster_mid.reshape(1, PTS),
        cluster_coarse.reshape(1, PTS),
        near_weight,
        up_weights,
        down_weights,
    )


def solution(mesh):
    rows = P(("gx", "gy"), None)
    flat = P(("gx", "gy"))
    size_x, size_y = mesh.shape["gx"], mesh.shape["gy"]
    return jax.shard_map(
        functools.partial(on_device, size_x, size_y),
        mesh=mesh,
        in_specs=(rows, rows, rows, rows, rows, flat, flat, flat, P(), P(), P()),
        out_specs=(rows, rows, P()),
        check_vma=False,
    )
```

time: 2080 us -> 76.8 us (0.04)
  the two profiles are of different devices: /device:TPU:2 before, /device:TPU:1 now
where the time goes in v1:
time: 76.8 us; the launch traced here: 76.4 us
  Pallas kernels  66.7 us (87%)
  local copies, waits for them, and re-layouts  9.07 us (12%)
    pallas_call x1, Pallas kernels, on_device(): pl.pallas_call(functools.partial(kernel, size_x, size_y), out_shape=(jax....  66.7 us
    unnamed x25, local copies, waits for them, and re-layouts  9.07 us

profile of v1, /device:TPU:1, one launch (start us, length us, event | category | flops | bytes accessed | tf_op | source)
XLA Modules:
  0.0 76.4 jit_solution(5679199893728239932)
XLA Ops:
  0.6 0.0 copy-start.10
  0.6 0.0 copy-start.9
  0.7 0.0 copy-start.8
  0.7 0.0 copy-start.7
  0.7 0.6 copy-done.10
  1.3 0.0 copy-done.9
  1.3 0.0 copy-done.8
  1.3 0.0 copy-done.7
  1.4 0.0 copy-start
  1.4 1.0 %copy-done = bf16[512,384]{1,0:T(8,128)(2,1)S(1)} copy-done((bf16[512,384]{1,0:T(8,128)(2,1)S(1)}, bf16[512,384]{1,0:T(8,128)(2,1)}, u32[]{:S(2)}) %copy-start) | copy-done | bytes 393240
  2.4 0.0 copy-start.1
  2.4 0.9 %copy-done.1 = bf16[1024,128]{1,0:T(8,128)(2,1)S(1)} copy-done((bf16[1024,128]{1,0:T(8,128)(2,1)S(1)}, bf16[1024,128]{1,0:T(8,128)(2,1)}, u32[]{:S(2)}) %copy-start.1) | copy-done | bytes 262168
  3.3 0.0 copy-start.2
  3.3 0.9 %copy-done.2 = bf16[512,128]{1,0:T(8,128)(2,1)S(1)} copy-done((bf16[512,128]{1,0:T(8,128)(2,1)S(1)}, bf16[512,128]{1,0:T(8,128)(2,1)}, u32[]{:S(2)}) %copy-start.2) | copy-done | bytes 131096
  4.2 0.0 copy-start.3
  4.2 0.9 %copy-done.3 = bf16[512,128]{1,0:T(8,128)(2,1)S(1)} copy-done((bf16[512,128]{1,0:T(8,128)(2,1)S(1)}, bf16[512,128]{1,0:T(8,128)(2,1)}, u32[]{:S(2)}) %copy-start.3) | copy-done | bytes 131096
  5.1 0.0 copy-start.4
  5.1 0.9 %copy-done.4 = bf16[3,128,128]{2,1,0:T(8,128)(2,1)S(1)} copy-done((bf16[3,128,128]{2,1,0:T(8,128)(2,1)S(1)}, bf16[3,128,128]{2,1,0:T(8,128)(2,1)}, u32[]{:S(2)}) %copy-start.4) | copy-done | bytes 98328
  6.0 0.0 copy-start.5
  6.0 0.9 %copy-done.5 = bf16[3,128,128]{2,1,0:T(8,128)(2,1)S(1)} copy-done((bf16[3,128,128]{2,1,0:T(8,128)(2,1)S(1)}, bf16[3,128,128]{2,1,0:T(8,128)(2,1)}, u32[]{:S(2)}) %copy-start.5) | copy-done | bytes 98328
  6.9 0.0 copy-start.6
  6.9 0.8 copy-done.6
  7.7 66.7 %layer.1 = (bf16[512,128]{1,0:T(8,128)(2,1)S(1)}, bf16[512,128]{1,0:T(8,128)(2,1)S(1)}, f32[7,128,128]{2,1,0:T(8,128)S(1)}) custom-call(bf16[4,128,128]{2,1,0:T(8,128)(2,1)S(1)} %bitcast.6, bf16[512,128]{1,0:T(8,128)(2,1)S(1)} %copy-done.3, bf16[512,384]{1,0:T(8,128)(2,1)S(1)} %copy-done, s32[4,3]{1,0:T(4,128)S(1)} %copy-done.7, ...), custom_call_target="tpu_custom_call" | custom-call | tf_op jit(solution)/shard_map/layer/pallas_call | solution.py:471
  74.3 0.7 copy.17
  75.0 0.7 copy.18
  75.7 0.8 %copy.19 = f32[7,128,128]{2,1,0:T(8,128)} copy(f32[7,128,128]{2,1,0:T(8,128)S(1)} %get-tuple-element.8) | data formatting | bytes 917504
Async XLA Ops:
  0.6 0.7 copy-start.10
  0.6 0.7 copy-start.9
  0.7 0.7 copy-start.8
  0.7 0.7 copy-start.7
  1.4 1.0 %copy-start = (bf16[512,384]{1,0:T(8,128)(2,1)S(1)}, bf16[512,384]{1,0:T(8,128)(2,1)}, u32[]{:S(2)}) copy-start(bf16[512,384]{1,0:T(8,128)(2,1)} %tiles_ref.1) | copy-start | bytes 1179652
  2.4 0.9 %copy-start.1 = (bf16[1024,128]{1,0:T(8,128)(2,1)S(1)}, bf16[1024,128]{1,0:T(8,128)(2,1)}, u32[]{:S(2)}) copy-start(bf16[1024,128]{1,0:T(8,128)(2,1)} %param.15) | copy-start | bytes 786436
  3.3 0.9 %copy-start.2 = (bf16[512,128]{1,0:T(8,128)(2,1)S(1)}, bf16[512,128]{1,0:T(8,128)(2,1)}, u32[]{:S(2)}) copy-start(bf16[512,128]{1,0:T(8,128)(2,1)} %param.11) | copy-start | bytes 393220
  4.2 0.9 %copy-start.3 = (bf16[512,128]{1,0:T(8,128)(2,1)S(1)}, bf16[512,128]{1,0:T(8,128)(2,1)}, u32[]{:S(2)}) copy-start(bf16[512,128]{1,0:T(8,128)(2,1)} %cot_ref.1) | copy-start | bytes 393220
  5.1 0.9 %copy-start.4 = (bf16[3,128,128]{2,1,0:T(8,128)(2,1)S(1)}, bf16[3,128,128]{2,1,0:T(8,128)(2,1)}, u32[]{:S(2)}) copy-start(bf16[3,128,128]{2,1,0:T(8,128)(2,1)} %up_ref.1) | copy-start | bytes 294916
  6.0 0.9 %copy-start.5 = (bf16[3,128,128]{2,1,0:T(8,128)(2,1)S(1)}, bf16[3,128,128]{2,1,0:T(8,128)(2,1)}, u32[]{:S(2)}) copy-start(bf16[3,128,128]{2,1,0:T(8,128)(2,1)} %dn_ref.1) | copy-start | bytes 294916
  6.9 0.8 copy-start.6

commit v2 on v1

--- a/solution.py
+++ b/solution.py
@@ -47,6 +47,24 @@
 def kernel(
     size_x,
     size_y,
+    pts_in,
+    cot_in,
+    tiles_in,
+    src_in,
+    halo_in,
+    c0_in,
+    c1_in,
+    c2_in,
+    nw_in,
+    up_in,
+    dn_in,
+    mixed_out,
+    pg_out,
+    wg_out,
+    mixed_ref,
+    pg_ref,
+    wg_ref,
+    out_sem,
     pts_ref,
     cot_ref,
     tiles_ref,
@@ -58,9 +76,7 @@
     nw_ref,
     up_ref,
     dn_ref,
-    mixed_ref,
-    pg_ref,
-    wg_ref,
+    load_sem,
     ot0,
     ot1,
     ot2,
@@ -86,8 +102,12 @@
     r_u1,
     z_u1,
     u1,
-    n0all,
-    sg0all,
+    ut0,
+    u0_t,
+    cat0,
+    cat1,
+    group,
+    group_bf,
     s_p2,
     r_p2,
     z_p2,
@@ -100,6 +120,8 @@
     recv_sem,
     halo_send,
     halo_recv,
+    ids_recv,
+    relay,
 ):
     size_z = size_x // 2
     size_q = 2 * size_y
@@ -124,14 +146,14 @@
 
     count = {"y": size_y, "z": size_z, "q": size_q}
 
-    def exchange(kind, step, source, target):
+    def exchange(kind, step, source, target, landed=None):
         def body(o, carry):
             i, device = peer(kind, o)
             pltpu.make_async_remote_copy(
                 src_ref=source(i),
                 dst_ref=target,
                 send_sem=send_sem.at[step],
-                recv_sem=recv_sem.at[step],
+                recv_sem=recv_sem.at[step] if landed is None else landed,
                 device_id=device,
                 device_id_type=MESH,
             ).start()
@@ -142,24 +164,53 @@
     def arrived(step, ref):
         pltpu.make_async_copy(ref, ref, recv_sem.at[step]).wait()
 
+    def id_arrived(i):
+        pltpu.make_async_copy(ids.at[i], ids.at[i], ids_recv.at[i]).wait()
+
     def sent(step, ref):
         pltpu.make_async_copy(ref, ref, send_sem.at[step]).wait()
 
+    loads = {
+        name: pltpu.make_async_copy(source, target, load_sem.at[i])
+        for i, (name, source, target) in enumerate(
+            (
+                ("c0", c0_in, c0_ref),
+                ("pts", pts_in, pts_ref),
+                ("cot", cot_in, cot_ref),
+                ("c1", c1_in, c1_ref),
+                ("c2", c2_in, c2_ref),
+                ("nw", nw_in, nw_ref),
+                ("src", src_in, src_ref),
+                ("tiles", tiles_in, tiles_ref),
+                ("halo", halo_in, halo_ref),
+                ("up", up_in, up_ref),
+                ("dn", dn_in, dn_ref),
+            )
+        )
+    }
+    for load in loads.values():
+        load.start()
+
     barrier = pltpu.get_barrier_semaphore()
 
-    def greet(kind):
+    reach = size_z // 4
+
+    def greet(kind, steps, shift):
         def body(o, carry):
-            _, device = peer(kind, o)
+            _, device = peer(kind, o + shift)
             pl.semaphore_signal(barrier, inc=1, device_id=device, device_id_type=MESH)
             return carry
 
-        lax.fori_loop(1, count[kind], body, 0)
-
-    greet("z")
-    greet("q")
+        lax.fori_loop(1, steps + 1, body, 0)
+
+    greet("z", reach, 0)
+    greet("z", reach, size_z - reach - 1)
+    greet("q", size_q - 1, 0)
     beside = lax.rem(a + size_x - 1 + 2 * core, size_x)
     pl.semaphore_signal(barrier, inc=1, device_id=(beside, b), device_id_type=MESH)
 
+    for name in ("c0", "pts", "cot", "c1", "c2"):
+        loads[name].wait()
     points = pts_ref[...].reshape(PTS, C)
     cot = cot_ref[...]
     c0, c1, c2 = c0_ref[...], c1_ref[...], c2_ref[...]
@@ -178,6 +229,8 @@
     s_p1[:k2, C:] = jnp.where(lane < k2, counts[:k2], pltpu.roll(t2, C - k2, 1)).astype(BF16)
     s_p1[k2 : 2 * k2, C:] = jnp.where(lane < k2, counts[k2 : 2 * k2], t2).astype(BF16)
 
+    for name in ("nw", "src", "tiles", "halo", "up", "dn"):
+        loads[name].wait()
     near_grad = dot(cot, nw_ref[...], NT).astype(BF16)
     returned = [jnp.zeros((BLK, C), F32)] * 4
     for t in range(4):
@@ -196,9 +249,12 @@
     for s in range(4):
         ret[s] = returned[s]
 
-    pl.semaphore_wait(barrier, size_z - 1 + size_q - 1 + 1)
-
-    exchange("y", 0, lambda i: ids.at[b], ids.at[b])
+    pl.semaphore_wait(barrier, 2 * reach + size_q - 1 + 1)
+    for o in (reach, size_z - reach):
+        _, device = peer("z", o)
+        pl.semaphore_signal(relay, inc=1, device_id=device, device_id_type=MESH)
+
+    exchange("y", 0, lambda i: ids.at[b], ids.at[b], ids_recv.at[b])
     exchange("y", 1, lambda i: s_u0.at[pl.ds(i * OWN0, OWN0)], r_u0.at[b])
     exchange("q", 2, lambda i: s_p1.at[pl.ds(i * 16, 16)], r_p1.at[q])
     exchange("y", 3, lambda i: s_t0.at[pl.ds(i * OWN0, OWN0)], r_t0.at[b])
@@ -229,16 +285,35 @@
                         device_id_type=MESH,
                     ).start()
 
-    arrived(0, ids.at[pl.ds(0, size_y - 1)])
+    side_y = math.isqrt(size_y)
+    near_first = sorted(
+        ((dx, dy) for dx in range(side_y) for dy in range(size_y // side_y)),
+        key=lambda d: min(d[0], side_y - d[0]) + min(d[1], size_y // side_y - d[1]),
+    )
+    fines = []
     pair_counts = jnp.zeros((OWN0, k1), F32)
-    for i in range(size_y):
+    for n, (dx, dy) in enumerate(near_first):
+        per = size_y // side_y
+        i = lax.rem(lax.div(b, per) + dx, side_y) * per + lax.rem(lax.rem(b, per) + dy, per)
+        if n > 0:
+            id_arrived(i)
         packed = ids[i]
         fine = lax.shift_right_logical(packed, 10)
         mid = lax.bitwise_and(packed, 1023)
-        pair_counts = pair_counts + dot(
-            one_hot_rows(fine, b * OWN0, OWN0), one_hot_rows(mid, 0, k1), NT
-        )
+        fines.append(fine)
+        here = slice(n * PTS, (n + 1) * PTS)
+        cat1[:, here] = one_hot_rows(mid, 0, k1)
+        pair_counts = pair_counts + dot(one_hot_rows(fine, b * OWN0, OWN0), cat1[:, here], NT)
     pair_counts = pair_counts.astype(BF16)
+
+    def group_counts(first, last):
+        for n in range(first, last):
+            cat0[:, (n - first) * PTS : (n - first + 1) * PTS] = one_hot_rows(fines[n], 0, OWN0 * size_y)
+        part = dot(cat0[:, : (last - first) * PTS], cat1[:, first * PTS : last * PTS], NT)
+        if first == 0:
+            group[...] = part
+        else:
+            group[...] += part
 
     r_u0[b] = s_u0[pl.ds(pl.multiple_of(b * OWN0, OWN0), OWN0), :]
     arrived(1, r_u0.at[pl.ds(0, size_y - 1)])
@@ -250,18 +325,19 @@
     s_u1[...] = dot(pair_counts, n0, TN).astype(BF16)
     exchange("q", 4, lambda i: s_u1.at[pl.ds(i * 16, 16)], r_u1.at[q])
     mine32 = pl.ds(pl.multiple_of(b * OWN0, OWN0), OWN0)
-    n0all[mine32, :] = n0
-    exchange("y", 5, lambda i: n0all.at[mine32], n0all.at[mine32])
+    r_t0[b] = s_t0[mine32, :]
+    arrived(3, r_t0.at[pl.ds(0, size_y - 1)])
+    t0 = jnp.sum(r_t0[...].astype(F32), axis=0)
+    ut0[mine32, :C] = u0.astype(BF16)
+    ut0[mine32, C:] = t0.astype(BF16)
+    exchange("y", 5, lambda i: ut0.at[mine32], ut0.at[mine32])
 
     mine16 = pl.ds(pl.multiple_of(q * 16, 16), 16)
     r_p1[q] = s_p1[mine16, :]
     arrived(2, r_p1.at[pl.ds(0, size_q - 1)])
     z_p1[z] = jnp.sum(r_p1[...].astype(F32), axis=0).astype(BF16)
+    pl.semaphore_wait(relay, 2)
     exchange("z", 6, lambda i: z_p1.at[z], z_p1.at[z])
-
-    r_t0[b] = s_t0[mine32, :]
-    arrived(3, r_t0.at[pl.ds(0, size_y - 1)])
-    t0 = jnp.sum(r_t0[...].astype(F32), axis=0)
 
     for side in range(4):
         got = (
@@ -294,24 +370,39 @@
     ).astype(BF16)
     exchange("q", 7, lambda i: s_p2.at[lax.rem(i, size_y)], r_p2.at[q])
 
+    third = (size_y + 2) // 3
+    group_counts(0, third)
+
     r_u1[q] = s_u1[mine16, :]
     arrived(4, r_u1.at[pl.ds(0, size_q - 1)])
     z_u1[z] = jnp.sum(r_u1[...].astype(F32), axis=0).astype(BF16)
     exchange("z", 8, lambda i: z_u1.at[z], z_u1.at[z])
 
-    arrived(6, z_p1.at[pl.ds(0, size_z - 1)])
-    p1[mine16, :] = jnp.sum(z_p1[...].astype(F32), axis=0).astype(BF16)
-    exchange("q", 9, lambda i: p1.at[mine16], p1.at[mine16])
-
     r_p2[q] = s_p2[b]
     arrived(7, r_p2.at[pl.ds(0, size_q - 1)])
     z_p2[z] = jnp.sum(r_p2[...].astype(F32), axis=0).astype(BF16)
     exchange("z", 10, lambda i: z_p2.at[z], z_p2.at[z])
+    group_counts(third, 2 * third)
+
+    arrived(6, z_p1.at[pl.ds(0, size_z - 1)])
+    p1[mine16, :] = jnp.sum(z_p1[...].astype(F32), axis=0).astype(BF16)
+    exchange("q", 9, lambda i: p1.at[mine16], p1.at[mine16])
+
+    group_counts(2 * third, size_y)
+    group_bf[...] = group[...].astype(BF16)
+    arrived(5, ut0.at[pl.ds(0, (size_y - 1) * OWN0)])
+    u0_t[...] = ut0[:, :C].astype(F32).T.astype(BF16)
+    summed0 = dot(ut0[:, :C], up_ref[0])
+    inverse0 = inverse_rms(summed0)
+    normed0 = summed0 * inverse0
+    raw0 = dot(ut0[:, C:], dn_ref[0], NT)
 
     arrived(8, z_u1.at[pl.ds(0, size_z - 1)])
     u1[mine16, :] = jnp.sum(z_u1[...].astype(F32), axis=0).astype(BF16)
     exchange("q", 11, lambda i: u1.at[mine16], u1.at[mine16])
 
+    combined = points.astype(F32) + dot(nv[...], nw_ref[...])
+    combined = combined + dot(dot(ot0[...], normed0.astype(BF16), TN).astype(BF16), dn_ref[0])
     arrived(10, z_p2.at[pl.ds(0, size_z - 1)])
     g_p2[b] = jnp.sum(z_p2[...].astype(F32), axis=0) * scale
     exchange("y", 12, lambda i: g_p2.at[b], g_p2.at[b])
@@ -322,55 +413,66 @@
     t2 = jnp.where(lane < k2, pltpu.roll(upper_part, C - k2, 1), p1[k2 : 2 * k2, C:].astype(F32))
     t2 = t2.astype(BF16)
     counts = p1[:, C:][:, :k2]
+    counts_t = counts.astype(F32).T.astype(BF16)
 
     raw2 = dot(t2, dn_ref[2], NT)
     raw1 = dot(t1, dn_ref[1], NT)
-    raw0 = dot_split(t0, dn_ref[0], NT)
     arrived(11, u1.at[pl.ds(0, (size_q - 1) * 16)])
     summed1 = dot(u1[...], up_ref[1])
     inverse1 = inverse_rms(summed1)
     normed1 = summed1 * inverse1
     n1 = normed1.astype(BF16)
-    u2 = dot(counts, n1, TN)
+    u2 = dot(counts_t, n1)
     summed2 = dot_split(u2, up_ref[2])
     inverse2 = inverse_rms(summed2)
     normed2 = summed2 * inverse2
     n2 = normed2.astype(BF16)
     sg2 = norm_back(raw2, normed2, inverse2).astype(BF16)
-    raw1 = raw1 + dot_split(dot(counts, sg2), up_ref[2], NT)
+    back2 = dot(sg2, up_ref[2], NT)
+    back2_high = back2.astype(BF16)
+    back2_low = (back2 - back2_high.astype(F32)).astype(BF16)
+    raw1 = raw1 + dot(counts, back2_high) + dot(counts, back2_low)
     sg1 = norm_back(raw1, normed1, inverse1).astype(BF16)
-    raw0 = raw0 + dot_split(dot(pair_counts, sg1), up_ref[1], NT)
+    raw0 = raw0 + dot_split(dot(group_bf[...], sg1), up_ref[1], NT)
     sg0 = norm_back(raw0, normed0, inverse0).astype(BF16)
-    s_d[...] = dot_split(u0, sg0, TN).reshape(size_y, 8, C)
-    exchange("q", 13, lambda i: s_d.at[lax.rem(i, size_y)], r_d.at[q])
-    sg0all[mine32, :] = sg0
-    exchange("y", 14, lambda i: sg0all.at[mine32], sg0all.at[mine32])
+    s_d[...] = dot(u0_t[...], sg0).reshape(size_y, 8, C)
+    to_pair = pltpu.make_async_remote_copy(
+        src_ref=s_d.at[b],
+        dst_ref=r_d,
+        send_sem=send_sem.at[13],
+        recv_sem=recv_sem.at[13],
+        device_id=(a + 1 - 2 * core, b),
+        device_id_type=MESH,
+    )
+    to_pair.start()
 
     wg_ref[2] = dot(u1[...], sg1, TN) * scale
     wg_ref[3] = dot_split(u2, sg2, TN) * scale
+    to_pair.wait()
+    z_d[z] = s_d[b] + r_d[...]
+    exchange("z", 15, lambda i: z_d.at[z], z_d.at[z])
     wg_ref[5] = dot(n1, t1, TN) * scale
     wg_ref[6] = dot(n2, t2, TN) * scale
 
-    arrived(5, n0all.at[pl.ds(0, (size_y - 1) * OWN0)])
-    combined = points.astype(F32) + dot(nv[...], nw_ref[...])
-    combined = combined + dot(dot(ot0[...], n0all[...], TN).astype(BF16), dn_ref[0])
     combined = combined + dot(dot(ot1[...], n1, TN).astype(BF16), dn_ref[1])
     combined = combined + dot(dot(ot2[:k2, :], n2, TN).astype(BF16), dn_ref[2])
     mixed_ref[...] = combined.astype(BF16)
-
-    r_d[q] = s_d[b]
-    arrived(13, r_d.at[pl.ds(0, size_q - 1)])
-    z_d[z] = jnp.sum(r_d[...], axis=0)
-    exchange("z", 15, lambda i: z_d.at[z], z_d.at[z])
-
-    arrived(14, sg0all.at[pl.ds(0, (size_y - 1) * OWN0)])
-    upper0 = dot(ot0[...], sg0all[...], TN).astype(BF16)
+    put_mixed = pltpu.make_async_copy(mixed_ref, mixed_out, out_sem.at[0])
+    put_mixed.start()
+
+    upper0 = dot(ot0[...], sg0, TN).astype(BF16)
     grad = cot.astype(F32) + ret[...].reshape(PTS, C) + dot(upper0, up_ref[0], NT)
     pg_ref[...] = grad.astype(BF16)
+    put_pg = pltpu.make_async_copy(pg_ref, pg_out, out_sem.at[1])
+    put_pg.start()
 
     arrived(12, g_p2.at[pl.ds(0, size_y - 1)])
     wg_ref[0] = g_p2[:, :8, :].reshape(C, C)
     wg_ref[4] = g_p2[:, 8:, :].reshape(C, C)
+    put_first = pltpu.make_async_copy(wg_ref.at[0], wg_out.at[0], out_sem.at[2])
+    put_first.start()
+    put_rest = pltpu.make_async_copy(wg_ref.at[pl.ds(2, 5)], wg_out.at[pl.ds(2, 5)], out_sem.at[3])
+    put_rest.start()
 
     arrived(15, z_d.at[pl.ds(0, size_z - 1)])
     g_d[b] = jnp.sum(z_d[...], axis=0) * scale
@@ -381,7 +483,7 @@
         (2, r_p1.at[pl.ds(0, size_q - 1)]),
         (3, r_t0.at[pl.ds(0, size_y - 1)]),
         (4, r_u1.at[pl.ds(0, size_q - 1)]),
-        (5, n0all.at[pl.ds(0, (size_y - 1) * OWN0)]),
+        (5, ut0.at[pl.ds(0, (size_y - 1) * OWN0)]),
         (6, z_p1.at[pl.ds(0, size_z - 1)]),
         (7, r_p2.at[pl.ds(0, size_q - 1)]),
         (8, z_u1.at[pl.ds(0, size_z - 1)]),
@@ -389,8 +491,6 @@
         (10, z_p2.at[pl.ds(0, size_z - 1)]),
         (11, u1.at[pl.ds(0, (size_q - 1) * 16)]),
         (12, g_p2.at[pl.ds(0, size_y - 1)]),
-        (13, r_d.at[pl.ds(0, size_q - 1)]),
-        (14, sg0all.at[pl.ds(0, (size_y - 1) * OWN0)]),
         (15, z_d.at[pl.ds(0, size_z - 1)]),
     ):
         sent(step, ref)
@@ -402,9 +502,27 @@
                 two = fx.at[pl.ds(0, 2)]
                 pltpu.make_async_copy(two, two, halo_send.at[2 * side + kind]).wait()
 
+    for put in (put_mixed, put_pg, put_first, put_rest):
+        put.wait()
     arrived(16, g_d.at[pl.ds(0, size_y - 1)])
     sent(16, g_d.at[pl.ds(0, size_y - 1)])
     wg_ref[1] = g_d[...].reshape(C, C)
+    put_last = pltpu.make_async_copy(wg_ref.at[1], wg_out.at[1], out_sem.at[4])
+    put_last.start()
+    put_last.wait()
+
+
+def store(*refs):
+    sources, targets, held, sem = refs[:3], refs[3:6], refs[6:9], refs[9]
+    first = [pltpu.make_async_copy(sources[i], held[i], sem.at[i]) for i in range(3)]
+    then = [pltpu.make_async_copy(held[i], targets[i], sem.at[3 + i]) for i in range(3)]
+    for copy in first:
+        copy.start()
+    for i in range(3):
+        first[i].wait()
+        then[i].start()
+    for copy in then:
+        copy.wait()
 
 
 def on_device(
@@ -423,11 +541,26 @@
     down_weights,
 ):
     size_z, size_q, k1 = size_x // 2, 2 * size_y, size_x * size_y
-    vmem = pl.BlockSpec(memory_space=pltpu.VMEM)
-    smem = pl.BlockSpec(memory_space=pltpu.SMEM)
     k0 = OWN0 * size_y
     blocks = pltpu.VMEM((4, BLK, C), BF16)
+    hbm = pl.BlockSpec(memory_space=pltpu.HBM)
     scratch = [
+        pltpu.VMEM((PTS, C), BF16),
+        pltpu.VMEM((PTS, C), BF16),
+        pltpu.VMEM((7, C, C), F32),
+        pltpu.SemaphoreType.DMA((5,)),
+        pltpu.VMEM((4, BLK, C), BF16),
+        pltpu.VMEM((PTS, C), BF16),
+        pltpu.VMEM((PTS, 3 * BLK), BF16),
+        pltpu.SMEM((4, 3), jnp.int32),
+        pltpu.VMEM((8, BLK, BLK), BF16),
+        pltpu.VMEM((1, PTS), jnp.int32),
+        pltpu.VMEM((1, PTS), jnp.int32),
+        pltpu.VMEM((1, PTS), jnp.int32),
+        pltpu.VMEM((C, C), BF16),
+        pltpu.VMEM((3, C, C), BF16),
+        pltpu.VMEM((3, C, C), BF16),
+        pltpu.SemaphoreType.DMA((11,)),
         pltpu.VMEM((k0, PTS), BF16),
         pltpu.VMEM((k1, PTS), BF16),
         pltpu.VMEM((C, PTS), BF16),
@@ -453,34 +586,40 @@
         pltpu.VMEM((size_q, 16, C), BF16),
         pltpu.VMEM((size_z, 16, C), BF16),
         pltpu.VMEM((k1, C), BF16),
-        pltpu.VMEM((k0, C), BF16),
-        pltpu.VMEM((k0, C), BF16),
+        pltpu.VMEM((k0, 2 * C), BF16),
+        pltpu.VMEM((C, k0), BF16),
+        pltpu.VMEM((k0, (size_y + 2) // 3 * PTS), BF16),
+        pltpu.VMEM((k1, size_y * PTS), BF16),
+        pltpu.VMEM((k0, k1), F32),
+        pltpu.VMEM((k0, k1), BF16),
         pltpu.VMEM((size_y, 16, C), BF16),
         pltpu.VMEM((size_q, 16, C), BF16),
         pltpu.VMEM((size_z, 16, C), BF16),
         pltpu.VMEM((size_y, 16, C), F32),
         pltpu.VMEM((size_y, 8, C), F32),
-        pltpu.VMEM((size_q, 8, C), F32),
+        pltpu.VMEM((8, C), F32),
         pltpu.VMEM((size_z, 8, C), F32),
         pltpu.VMEM((size_y, 8, C), F32),
         pltpu.SemaphoreType.DMA((17,)),
         pltpu.SemaphoreType.DMA((17,)),
         pltpu.SemaphoreType.DMA((8,)),
         pltpu.SemaphoreType.DMA((8,)),
+        pltpu.SemaphoreType.DMA((size_y,)),
+        pltpu.SemaphoreType.REGULAR,
     ]
-    return pl.pallas_call(
+    outs = pl.pallas_call(
         functools.partial(kernel, size_x, size_y),
         out_shape=(
             jax.ShapeDtypeStruct((PTS, C), BF16),
             jax.ShapeDtypeStruct((PTS, C), BF16),
             jax.ShapeDtypeStruct((7, C, C), F32),
         ),
-        in_specs=[vmem, vmem, vmem, smem, vmem, vmem, vmem, vmem, vmem, vmem, vmem],
-        out_specs=(vmem, vmem, vmem),
+        in_specs=[hbm] * 11,
+        out_specs=(hbm,) * 3,
         scratch_shapes=scratch,
         name="layer",
         compiler_params=pltpu.CompilerParams(
-            collective_id=0, has_side_effects=True, vmem_limit_bytes=48 * 1024 * 1024
+            collective_id=0, has_side_effects=True, vmem_limit_bytes=60 * 1024 * 1024
         ),
     )(
         points.reshape(4, BLK, C),
@@ -495,6 +634,15 @@
         up_weights,
         down_weights,
     )
+    return pl.pallas_call(
+        store,
+        out_shape=tuple(jax.ShapeDtypeStruct(o.shape, o.dtype) for o in outs),
+        in_specs=[hbm] * 3,
+        out_specs=(hbm,) * 3,
+        scratch_shapes=[pltpu.VMEM(o.shape, o.dtype) for o in outs] + [pltpu.SemaphoreType.DMA((6,))],
+        name="store",
+        compiler_params=pltpu.CompilerParams(vmem_limit_bytes=60 * 1024 * 1024),
+    )(*outs)
 
 
 def solution(mesh):

time: 76.8 us -> 67.2 us (0.88)
  local copies, waits for them, and re-layouts: 9.07 us -> 0 us
    unnamed x25 -> x0, local copies, waits for them, and re-layouts: 9.07 us -> none
    pallas_call x1, Pallas kernels: 66.7 us -> 64.3 us  [on_device(): pl.pallas_call(functools.partial(kernel, size_x, size_y), out_shape=(jax....]
    pallas_call x0 -> x1, Pallas kernels: none -> 1.97 us  [on_device(): pl.pallas_call(store, out_shape=tuple((jax.ShapeDtypeStruct(o.shape, o.dt...]
where the time goes in v2:
time: 67.2 us; the launch traced here: 67 us
  Pallas kernels  66.2 us (99%)
  between operations  0.8 us (1%)
    pallas_call x1, Pallas kernels, on_device(): pl.pallas_call(functools.partial(kernel, size_x, size_y), out_shape=(jax....  64.3 us
    pallas_call x1, Pallas kernels, on_device(): pl.pallas_call(store, out_shape=tuple((jax.ShapeDtypeStruct(o.shape, o.dt...  1.97 us

profile of v2, /device:TPU:1, one launch (start us, length us, event | category | flops | bytes accessed | tf_op | source)
XLA Modules:
  0.0 67.0 jit_solution(11383437582193366580)
XLA Ops:
  0.6 64.3 %layer.1 = (bf16[512,128]{1,0:T(8,128)(2,1)}, bf16[512,128]{1,0:T(8,128)(2,1)}, f32[7,128,128]{2,1,0:T(8,128)}) custom-call(bf16[4,128,128]{2,1,0:T(8,128)(2,1)} %bitcast.6, bf16[512,128]{1,0:T(8,128)(2,1)} %cot_in.1, bf16[512,384]{1,0:T(8,128)(2,1)} %tiles_in.1, s32[4,3]{1,0:T(4,128)} %src_in.1, bf16[8,128,128]{2,1,0:T(8,128)(2,1)} %bitcast.5, ...), custom_call_target="tpu_custom_call" | custom-call | tf_op jit(solution)/shard_map/layer/pallas_call | solution.py:610
  64.9 2.0 %store.1 = (bf16[512,128]{1,0:T(8,128)(2,1)}, bf16[512,128]{1,0:T(8,128)(2,1)}, f32[7,128,128]{2,1,0:T(8,128)}) custom-call(bf16[512,128]{1,0:T(8,128)(2,1)} %get-tuple-element.6.refs_0_, bf16[512,128]{1,0:T(8,128)(2,1)} %get-tuple-element.7.refs_1_, f32[7,128,128]{2,1,0:T(8,128)} %get-tuple-element.8.refs_2_), custom_call_target="tpu_custom_call" | custom-call | tf_op jit(solution)/shard_map/store/pallas_call | solution.py:637

commit v3 on v2

--- a/solution.py
+++ b/solution.py
@@ -96,7 +96,8 @@
     r_t0,
     s_p1,
     r_p1,
-    z_p1,
+    n_p1,
+    f_p1,
     p1,
     s_u1,
     r_u1,
@@ -115,7 +116,6 @@
     s_d,
     r_d,
     z_d,
-    g_d,
     send_sem,
     recv_sem,
     halo_send,
@@ -141,10 +141,16 @@
         if kind == "z":
             i = lax.rem(z + o, size_z)
             return i, (i * 2 + core, b)
+        if kind == "near":
+            i = lax.rem(z + o, 4)
+            return i, ((z - lax.rem(z, 4) + i) * 2 + core, b)
+        if kind == "far":
+            i = lax.rem(z + 4 * o, size_z)
+            return lax.div(i, 4), (i * 2 + core, b)
         i = lax.rem(q + o, size_q)
         return i, (z * 2 + lax.div(i, size_y), lax.rem(i, size_y))
 
-    count = {"y": size_y, "z": size_z, "q": size_q}
+    count = {"y": size_y, "z": size_z, "q": size_q, "near": 4, "far": size_z // 4}
 
     def exchange(kind, step, source, target, landed=None):
         def body(o, carry):
@@ -188,9 +194,6 @@
             )
         )
     }
-    for load in loads.values():
-        load.start()
-
     barrier = pltpu.get_barrier_semaphore()
 
     reach = size_z // 4
@@ -208,6 +211,9 @@
     greet("q", size_q - 1, 0)
     beside = lax.rem(a + size_x - 1 + 2 * core, size_x)
     pl.semaphore_signal(barrier, inc=1, device_id=(beside, b), device_id_type=MESH)
+
+    for load in loads.values():
+        load.start()
 
     for name in ("c0", "pts", "cot", "c1", "c2"):
         loads[name].wait()
@@ -257,7 +263,6 @@
     exchange("y", 0, lambda i: ids.at[b], ids.at[b], ids_recv.at[b])
     exchange("y", 1, lambda i: s_u0.at[pl.ds(i * OWN0, OWN0)], r_u0.at[b])
     exchange("q", 2, lambda i: s_p1.at[pl.ds(i * 16, 16)], r_p1.at[q])
-    exchange("y", 3, lambda i: s_t0.at[pl.ds(i * OWN0, OWN0)], r_t0.at[b])
     has = (a > 0, a < size_x - 1, b > 0, b < size_y - 1)
 
     def halo_copies(side):
@@ -270,11 +275,14 @@
         return [[(pts_ref.at[i], fy.at[i - 1]) for i in (1, 3)], [(spy.at[i], by.at[i - 1]) for i in (1, 3)]]
 
     neighbour = ((a - 1, b), (a + 1, b), (a, b - 1), (a, b + 1))
-    for side in range(4):
-
-        @pl.when(has[side])
-        def _(side=side):
-            for kind in range(2):
+    landing = ((fx, bx, 0, 2), (fx, bx, 2, 4), (fy, by, 0, 2), (fy, by, 2, 4))
+    edge = ((0, 1), (2, 3), (0, 2), (1, 3))
+
+    def send_halo(kind):
+        for side in range(4):
+
+            @pl.when(has[side])
+            def _(side=side):
                 for source, target in halo_copies(side)[kind]:
                     pltpu.make_async_remote_copy(
                         src_ref=source,
@@ -284,6 +292,20 @@
                         device_id=neighbour[side],
                         device_id_type=MESH,
                     ).start()
+
+    def wait_halo(kind):
+        for side in range(4):
+            ref = landing[side][kind]
+
+            @pl.when(has[side])
+            def _(side=side, ref=ref):
+                two = ref.at[pl.ds(landing[side][2], 2)]
+                pltpu.make_async_copy(two, two, halo_recv.at[2 * side + kind]).wait()
+
+            @pl.when(jnp.logical_not(has[side]))
+            def _(side=side, ref=ref):
+                for i in edge[side]:
+                    ref[i] = jnp.zeros((BLK, C), BF16)
 
     side_y = math.isqrt(size_y)
     near_first = sorted(
@@ -325,44 +347,41 @@
     s_u1[...] = dot(pair_counts, n0, TN).astype(BF16)
     exchange("q", 4, lambda i: s_u1.at[pl.ds(i * 16, 16)], r_u1.at[q])
     mine32 = pl.ds(pl.multiple_of(b * OWN0, OWN0), OWN0)
+    exchange("y", 3, lambda i: s_t0.at[pl.ds(i * OWN0, OWN0)], r_t0.at[b])
+
+    mine16 = pl.ds(pl.multiple_of(q * 16, 16), 16)
+    r_p1[q] = s_p1[mine16, :]
+    arrived(2, r_p1.at[pl.ds(0, size_q - 1)])
+    z_near, z_far = lax.rem(z, 4), lax.div(z, 4)
+    n_p1[z_near] = jnp.sum(r_p1[...].astype(F32), axis=0).astype(BF16)
+    pl.semaphore_wait(relay, 2)
+    exchange("near", 6, lambda i: n_p1.at[z_near], n_p1.at[z_near])
+
+    third = (size_y + 2) // 3
+    group_counts(0, third)
+
+    arrived(6, n_p1.at[pl.ds(0, 3)])
+    f_p1[z_far] = jnp.sum(n_p1[...].astype(F32), axis=0).astype(BF16)
+    exchange("far", 14, lambda i: f_p1.at[z_far], f_p1.at[z_far])
+
+    r_u1[q] = s_u1[mine16, :]
+    arrived(4, r_u1.at[pl.ds(0, size_q - 1)])
+    z_u1[z] = jnp.sum(r_u1[...].astype(F32), axis=0).astype(BF16)
+    exchange("z", 8, lambda i: z_u1.at[z], z_u1.at[z])
+
     r_t0[b] = s_t0[mine32, :]
     arrived(3, r_t0.at[pl.ds(0, size_y - 1)])
     t0 = jnp.sum(r_t0[...].astype(F32), axis=0)
     ut0[mine32, :C] = u0.astype(BF16)
     ut0[mine32, C:] = t0.astype(BF16)
     exchange("y", 5, lambda i: ut0.at[mine32], ut0.at[mine32])
-
-    mine16 = pl.ds(pl.multiple_of(q * 16, 16), 16)
-    r_p1[q] = s_p1[mine16, :]
-    arrived(2, r_p1.at[pl.ds(0, size_q - 1)])
-    z_p1[z] = jnp.sum(r_p1[...].astype(F32), axis=0).astype(BF16)
-    pl.semaphore_wait(relay, 2)
-    exchange("z", 6, lambda i: z_p1.at[z], z_p1.at[z])
-
-    for side in range(4):
-        got = (
-            (fx.at[pl.ds(0, 2)], bx.at[pl.ds(0, 2)])
-            if side == 0
-            else (fx.at[pl.ds(2, 2)], bx.at[pl.ds(2, 2)])
-            if side == 1
-            else (fy.at[pl.ds(0, 2)], by.at[pl.ds(0, 2)])
-        )
-
-        @pl.when(has[side])
-        def _(side=side, got=got):
-            for kind in range(2):
-                pltpu.make_async_copy(got[kind], got[kind], halo_recv.at[2 * side + kind]).wait()
-
-        @pl.when(jnp.logical_not(has[side]))
-        def _(side=side):
-            for i in ((0, 1), (2, 3), (0, 2), (1, 3))[side]:
-                for ref in ((fx, bx) if side < 2 else (fy, by)):
-                    ref[i] = jnp.zeros((BLK, C), BF16)
-
+    send_halo(0)
+    group_counts(third, 2 * third)
+
+    wait_halo(0)
     for t in range(4):
         total = near[t] + dot(halo_ref[2 * t], fx[t]) + dot(halo_ref[2 * t + 1], fy[t])
         nv[pl.ds(t * BLK, BLK), :] = total.astype(BF16)
-        ret[t] = ret[t] + bx[t].astype(F32) + by[t].astype(F32)
     near_part = dot(nv[...], cot, TN)
     down0_part = dot(n0, t0.astype(BF16), TN)
     s_p2[...] = jnp.concatenate(
@@ -370,26 +389,6 @@
     ).astype(BF16)
     exchange("q", 7, lambda i: s_p2.at[lax.rem(i, size_y)], r_p2.at[q])
 
-    third = (size_y + 2) // 3
-    group_counts(0, third)
-
-    r_u1[q] = s_u1[mine16, :]
-    arrived(4, r_u1.at[pl.ds(0, size_q - 1)])
-    z_u1[z] = jnp.sum(r_u1[...].astype(F32), axis=0).astype(BF16)
-    exchange("z", 8, lambda i: z_u1.at[z], z_u1.at[z])
-
-    r_p2[q] = s_p2[b]
-    arrived(7, r_p2.at[pl.ds(0, size_q - 1)])
-    z_p2[z] = jnp.sum(r_p2[...].astype(F32), axis=0).astype(BF16)
-    exchange("z", 10, lambda i: z_p2.at[z], z_p2.at[z])
-    group_counts(third, 2 * third)
-
-    arrived(6, z_p1.at[pl.ds(0, size_z - 1)])
-    p1[mine16, :] = jnp.sum(z_p1[...].astype(F32), axis=0).astype(BF16)
-    exchange("q", 9, lambda i: p1.at[mine16], p1.at[mine16])
-
-    group_counts(2 * third, size_y)
-    group_bf[...] = group[...].astype(BF16)
     arrived(5, ut0.at[pl.ds(0, (size_y - 1) * OWN0)])
     u0_t[...] = ut0[:, :C].astype(F32).T.astype(BF16)
     summed0 = dot(ut0[:, :C], up_ref[0])
@@ -397,16 +396,18 @@
     normed0 = summed0 * inverse0
     raw0 = dot(ut0[:, C:], dn_ref[0], NT)
 
+    arrived(14, f_p1.at[pl.ds(0, size_z // 4 - 1)])
+    p1[mine16, :] = jnp.sum(f_p1[...].astype(F32), axis=0).astype(BF16)
+    exchange("q", 9, lambda i: p1.at[mine16], p1.at[mine16])
+
     arrived(8, z_u1.at[pl.ds(0, size_z - 1)])
     u1[mine16, :] = jnp.sum(z_u1[...].astype(F32), axis=0).astype(BF16)
     exchange("q", 11, lambda i: u1.at[mine16], u1.at[mine16])
 
+    group_counts(2 * third, size_y)
+    group_bf[...] = group[...].astype(BF16)
     combined = points.astype(F32) + dot(nv[...], nw_ref[...])
     combined = combined + dot(dot(ot0[...], normed0.astype(BF16), TN).astype(BF16), dn_ref[0])
-    arrived(10, z_p2.at[pl.ds(0, size_z - 1)])
-    g_p2[b] = jnp.sum(z_p2[...].astype(F32), axis=0) * scale
-    exchange("y", 12, lambda i: g_p2.at[b], g_p2.at[b])
-
     arrived(9, p1.at[pl.ds(0, (size_q - 1) * 16)])
     t1 = p1[:, :C]
     upper_part = p1[:k2, C:].astype(F32)
@@ -414,6 +415,11 @@
     t2 = t2.astype(BF16)
     counts = p1[:, C:][:, :k2]
     counts_t = counts.astype(F32).T.astype(BF16)
+
+    r_p2[q] = s_p2[b]
+    arrived(7, r_p2.at[pl.ds(0, size_q - 1)])
+    z_p2[z] = jnp.sum(r_p2[...].astype(F32), axis=0).astype(BF16)
+    exchange("z", 10, lambda i: z_p2.at[z], z_p2.at[z])
 
     raw2 = dot(t2, dn_ref[2], NT)
     raw1 = dot(t1, dn_ref[1], NT)
@@ -451,8 +457,13 @@
     to_pair.wait()
     z_d[z] = s_d[b] + r_d[...]
     exchange("z", 15, lambda i: z_d.at[z], z_d.at[z])
+    send_halo(1)
     wg_ref[5] = dot(n1, t1, TN) * scale
     wg_ref[6] = dot(n2, t2, TN) * scale
+
+    arrived(10, z_p2.at[pl.ds(0, size_z - 1)])
+    g_p2[b] = jnp.sum(z_p2[...].astype(F32), axis=0) * scale
+    exchange("y", 12, lambda i: g_p2.at[b], g_p2.at[b])
 
     combined = combined + dot(dot(ot1[...], n1, TN).astype(BF16), dn_ref[1])
     combined = combined + dot(dot(ot2[:k2, :], n2, TN).astype(BF16), dn_ref[2])
@@ -460,6 +471,9 @@
     put_mixed = pltpu.make_async_copy(mixed_ref, mixed_out, out_sem.at[0])
     put_mixed.start()
 
+    wait_halo(1)
+    for t in range(4):
+        ret[t] = ret[t] + bx[t].astype(F32) + by[t].astype(F32)
     upper0 = dot(ot0[...], sg0, TN).astype(BF16)
     grad = cot.astype(F32) + ret[...].reshape(PTS, C) + dot(upper0, up_ref[0], NT)
     pg_ref[...] = grad.astype(BF16)
@@ -475,8 +489,9 @@
     put_rest.start()
 
     arrived(15, z_d.at[pl.ds(0, size_z - 1)])
-    g_d[b] = jnp.sum(z_d[...], axis=0) * scale
-    exchange("y", 16, lambda i: g_d.at[b], g_d.at[b])
+    mine8 = pl.ds(pl.multiple_of(b * 8, 8), 8)
+    wg_ref[1, mine8, :] = jnp.sum(z_d[...], axis=0) * scale
+    exchange("y", 16, lambda i: wg_ref.at[1, mine8], wg_ref.at[1, mine8])
     for step, ref in (
         (0, ids.at[pl.ds(0, size_y - 1)]),
         (1, r_u0.at[pl.ds(0, size_y - 1)]),
@@ -484,7 +499,8 @@
         (3, r_t0.at[pl.ds(0, size_y - 1)]),
         (4, r_u1.at[pl.ds(0, size_q - 1)]),
         (5, ut0.at[pl.ds(0, (size_y - 1) * OWN0)]),
-        (6, z_p1.at[pl.ds(0, size_z - 1)]),
+        (6, n_p1.at[pl.ds(0, 3)]),
+        (14, f_p1.at[pl.ds(0, size_z // 4 - 1)]),
         (7, r_p2.at[pl.ds(0, size_q - 1)]),
         (8, z_u1.at[pl.ds(0, size_z - 1)]),
         (9, p1.at[pl.ds(0, (size_q - 1) * 16)]),
@@ -504,9 +520,8 @@
 
     for put in (put_mixed, put_pg, put_first, put_rest):
         put.wait()
-    arrived(16, g_d.at[pl.ds(0, size_y - 1)])
-    sent(16, g_d.at[pl.ds(0, size_y - 1)])
-    wg_ref[1] = g_d[...].reshape(C, C)
+    arrived(16, wg_ref.at[1, pl.ds(0, (size_y - 1) * 8)])
+    sent(16, wg_ref.at[1, pl.ds(0, (size_y - 1) * 8)])
     put_last = pltpu.make_async_copy(wg_ref.at[1], wg_out.at[1], out_sem.at[4])
     put_last.start()
     put_last.wait()
@@ -580,7 +595,8 @@
         pltpu.VMEM((size_y, OWN0, C), BF16),
         pltpu.VMEM((k1, 2 * C), BF16),
         pltpu.VMEM((size_q, 16, 2 * C), BF16),
-        pltpu.VMEM((size_z, 16, 2 * C), BF16),
+        pltpu.VMEM((4, 16, 2 * C), BF16),
+        pltpu.VMEM((size_z // 4, 16, 2 * C), BF16),
         pltpu.VMEM((k1, 2 * C), BF16),
         pltpu.VMEM((k1, C), BF16),
         pltpu.VMEM((size_q, 16, C), BF16),
@@ -599,7 +615,6 @@
         pltpu.VMEM((size_y, 8, C), F32),
         pltpu.VMEM((8, C), F32),
         pltpu.VMEM((size_z, 8, C), F32),
-        pltpu.VMEM((size_y, 8, C), F32),
         pltpu.SemaphoreType.DMA((17,)),
         pltpu.SemaphoreType.DMA((17,)),
         pltpu.SemaphoreType.DMA((8,)),

time: 67.2 us -> 65.5 us (0.975)
  the two profiles are of different devices: /device:TPU:1 before, /device:TPU:8 now
where the time goes in v3:
time: 65.5 us; the launch traced here: 65.3 us
  Pallas kernels  64.5 us (98%)
  between operations  0.8 us (1%)
    pallas_call x1, Pallas kernels, on_device(): pl.pallas_call(functools.partial(kernel, size_x, size_y), out_shape=(jax....  62.5 us
    pallas_call x1, Pallas kernels, on_device(): pl.pallas_call(store, out_shape=tuple((jax.ShapeDtypeStruct(o.shape, o.dt...  1.97 us

profile of v3, /device:TPU:8, one launch (start us, length us, event | category | flops | bytes accessed | tf_op | source)
XLA Modules:
  0.0 65.3 jit_solution(12899691380648486362)
XLA Ops:
  0.6 62.5 %layer.1 = (bf16[512,128]{1,0:T(8,128)(2,1)}, bf16[512,128]{1,0:T(8,128)(2,1)}, f32[7,128,128]{2,1,0:T(8,128)}) custom-call(bf16[4,128,128]{2,1,0:T(8,128)(2,1)} %bitcast.6, bf16[512,128]{1,0:T(8,128)(2,1)} %cot_in.1, bf16[512,384]{1,0:T(8,128)(2,1)} %tiles_in.1, s32[4,3]{1,0:T(4,128)} %src_in.1, bf16[8,128,128]{2,1,0:T(8,128)(2,1)} %bitcast.5, ...), custom_call_target="tpu_custom_call" | custom-call | tf_op jit(solution)/shard_map/layer/pallas_call | solution.py:625
  63.2 2.0 %store.1 = (bf16[512,128]{1,0:T(8,128)(2,1)}, bf16[512,128]{1,0:T(8,128)(2,1)}, f32[7,128,128]{2,1,0:T(8,128)}) custom-call(bf16[512,128]{1,0:T(8,128)(2,1)} %get-tuple-element.6.refs_0_, bf16[512,128]{1,0:T(8,128)(2,1)} %get-tuple-element.7.refs_1_, f32[7,128,128]{2,1,0:T(8,128)} %get-tuple-element.8.refs_2_), custom_call_target="tpu_custom_call" | custom-call | tf_op jit(solution)/shard_map/store/pallas_call | solution.py:652

commit v4 on v3

--- a/solution.py
+++ b/solution.py
@@ -134,9 +134,16 @@
     q = core * size_y + b
     scale = 1.0 / math.sqrt(PTS * size_x * size_y)
 
+    side_y = math.isqrt(size_y)
+    side_x = size_y // side_y
+
+    def in_plane(o):
+        x = lax.rem(lax.div(b, side_x) + lax.div(o, side_x), side_y)
+        return x * side_x + lax.rem(lax.rem(b, side_x) + lax.rem(o, side_x), side_x)
+
     def peer(kind, o):
         if kind == "y":
-            i = lax.rem(b + o, size_y)
+            i = in_plane(o)
             return i, (a, i)
         if kind == "z":
             i = lax.rem(z + o, size_z)
@@ -147,14 +154,24 @@
         if kind == "far":
             i = lax.rem(z + 4 * o, size_z)
             return lax.div(i, 4), (i * 2 + core, b)
-        i = lax.rem(q + o, size_q)
-        return i, (z * 2 + lax.div(i, size_y), lax.rem(i, size_y))
-
+        c = lax.rem(core + o, 2)
+        i = in_plane(lax.div(o, 2))
+        return c * size_y + i, (z * 2 + c, i)
+
+    farthest = {
+        "y": size_y // 2 + side_x // 2,
+        "z": size_z // 2,
+        "q": size_y + 2 * (side_x // 2),
+        "near": 2,
+        "far": size_z // 8,
+    }
     count = {"y": size_y, "z": size_z, "q": size_q, "near": 4, "far": size_z // 4}
 
     def exchange(kind, step, source, target, landed=None):
-        def body(o, carry):
-            i, device = peer(kind, o)
+        late = count[kind] - farthest[kind]
+
+        def body(k, carry):
+            i, device = peer(kind, jnp.where(k < late, k + farthest[kind], k - late + 1))
             pltpu.make_async_remote_copy(
                 src_ref=source(i),
                 dst_ref=target,
@@ -165,7 +182,7 @@
             ).start()
             return carry
 
-        lax.fori_loop(1, count[kind], body, 0)
+        lax.fori_loop(0, count[kind] - 1, body, 0)
 
     def arrived(step, ref):
         pltpu.make_async_copy(ref, ref, recv_sem.at[step]).wait()
@@ -278,8 +295,8 @@
     landing = ((fx, bx, 0, 2), (fx, bx, 2, 4), (fy, by, 0, 2), (fy, by, 2, 4))
     edge = ((0, 1), (2, 3), (0, 2), (1, 3))
 
-    def send_halo(kind):
-        for side in range(4):
+    def send_halo(kind, sides):
+        for side in sides:
 
             @pl.when(has[side])
             def _(side=side):
@@ -307,16 +324,17 @@
                 for i in edge[side]:
                     ref[i] = jnp.zeros((BLK, C), BF16)
 
-    side_y = math.isqrt(size_y)
+    send_halo(0, (0, 1))
+    send_halo(1, (0, 1))
+
     near_first = sorted(
-        ((dx, dy) for dx in range(side_y) for dy in range(size_y // side_y)),
-        key=lambda d: min(d[0], side_y - d[0]) + min(d[1], size_y // side_y - d[1]),
+        range(size_y),
+        key=lambda o: min(o // side_x, side_y - o // side_x) + min(o % side_x, side_x - o % side_x),
     )
     fines = []
     pair_counts = jnp.zeros((OWN0, k1), F32)
-    for n, (dx, dy) in enumerate(near_first):
-        per = size_y // side_y
-        i = lax.rem(lax.div(b, per) + dx, side_y) * per + lax.rem(lax.rem(b, per) + dy, per)
+    for n, o in enumerate(near_first):
+        i = in_plane(o)
         if n > 0:
             id_arrived(i)
         packed = ids[i]
@@ -375,7 +393,7 @@
     ut0[mine32, :C] = u0.astype(BF16)
     ut0[mine32, C:] = t0.astype(BF16)
     exchange("y", 5, lambda i: ut0.at[mine32], ut0.at[mine32])
-    send_halo(0)
+    send_halo(0, (2, 3))
     group_counts(third, 2 * third)
 
     wait_halo(0)
@@ -457,7 +475,7 @@
     to_pair.wait()
     z_d[z] = s_d[b] + r_d[...]
     exchange("z", 15, lambda i: z_d.at[z], z_d.at[z])
-    send_halo(1)
+    send_halo(1, (2, 3))
     wg_ref[5] = dot(n1, t1, TN) * scale
     wg_ref[6] = dot(n2, t2, TN) * scale
 
@@ -491,7 +509,9 @@
     arrived(15, z_d.at[pl.ds(0, size_z - 1)])
     mine8 = pl.ds(pl.multiple_of(b * 8, 8), 8)
     wg_ref[1, mine8, :] = jnp.sum(z_d[...], axis=0) * scale
-    exchange("y", 16, lambda i: wg_ref.at[1, mine8], wg_ref.at[1, mine8])
+    exchange("y", 16, lambda i: wg_ref.at[1, mine8], wg_out.at[1, mine8])
+    put_last = pltpu.make_async_copy(wg_ref.at[1, mine8], wg_out.at[1, mine8], out_sem.at[4])
+    put_last.start()
     for step, ref in (
         (0, ids.at[pl.ds(0, size_y - 1)]),
         (1, r_u0.at[pl.ds(0, size_y - 1)]),
@@ -518,24 +538,25 @@
                 two = fx.at[pl.ds(0, 2)]
                 pltpu.make_async_copy(two, two, halo_send.at[2 * side + kind]).wait()
 
-    for put in (put_mixed, put_pg, put_first, put_rest):
+    for put in (put_mixed, put_pg, put_first, put_rest, put_last):
         put.wait()
-    arrived(16, wg_ref.at[1, pl.ds(0, (size_y - 1) * 8)])
-    sent(16, wg_ref.at[1, pl.ds(0, (size_y - 1) * 8)])
-    put_last = pltpu.make_async_copy(wg_ref.at[1], wg_out.at[1], out_sem.at[4])
-    put_last.start()
-    put_last.wait()
+    arrived(16, wg_out.at[1, pl.ds(0, (size_y - 1) * 8)])
+    sent(16, wg_out.at[1, pl.ds(0, (size_y - 1) * 8)])
 
 
 def store(*refs):
     sources, targets, held, sem = refs[:3], refs[3:6], refs[6:9], refs[9]
-    first = [pltpu.make_async_copy(sources[i], held[i], sem.at[i]) for i in range(3)]
-    then = [pltpu.make_async_copy(held[i], targets[i], sem.at[3 + i]) for i in range(3)]
+    parts = [(2, pl.ds(i, 1)) for i in range(7)]
+    parts += [(n, pl.ds(i * BLK, BLK)) for n in (0, 1) for i in range(PTS // BLK)]
+    first, then = [], []
+    for p, (n, part) in enumerate(parts):
+        first.append(pltpu.make_async_copy(sources[n].at[part], held[n].at[part], sem.at[0, p]))
+        then.append(pltpu.make_async_copy(held[n].at[part], targets[n].at[part], sem.at[1, p]))
     for copy in first:
         copy.start()
-    for i in range(3):
-        first[i].wait()
-        then[i].start()
+    for p in range(len(parts)):
+        first[p].wait()
+        then[p].start()
     for copy in then:
         copy.wait()
 
@@ -654,7 +675,7 @@
         out_shape=tuple(jax.ShapeDtypeStruct(o.shape, o.dtype) for o in outs),
         in_specs=[hbm] * 3,
         out_specs=(hbm,) * 3,
-        scratch_shapes=[pltpu.VMEM(o.shape, o.dtype) for o in outs] + [pltpu.SemaphoreType.DMA((6,))],
+        scratch_shapes=[pltpu.VMEM(o.shape, o.dtype) for o in outs] + [pltpu.SemaphoreType.DMA((2, 15))],
         name="store",
         compiler_params=pltpu.CompilerParams(vmem_limit_bytes=60 * 1024 * 1024),
     )(*outs)

time: 65.5 us -> 65.3 us (level)
  the two profiles are of different devices: /device:TPU:8 before, /device:TPU:2 now
where the time goes in v4:
time: 65.3 us; the launch traced here: 65.1 us
  Pallas kernels  64.3 us (98%)
  between operations  0.8 us (1%)
    pallas_call x1, Pallas kernels, on_device(): pl.pallas_call(functools.partial(kernel, size_x, size_y), out_shape=(jax....  62.3 us
    pallas_call x1, Pallas kernels, on_device(): pl.pallas_call(store, out_shape=tuple((jax.ShapeDtypeStruct(o.shape, o.dt...  2.01 us

profile of v4, /device:TPU:2, one launch (start us, length us, event | category | flops | bytes accessed | tf_op | source)
XLA Modules:
  0.0 65.1 jit_solution(5984924025060972139)
XLA Ops:
  0.6 62.3 %layer.1 = (bf16[512,128]{1,0:T(8,128)(2,1)}, bf16[512,128]{1,0:T(8,128)(2,1)}, f32[7,128,128]{2,1,0:T(8,128)}) custom-call(bf16[4,128,128]{2,1,0:T(8,128)(2,1)} %bitcast.6, bf16[512,128]{1,0:T(8,128)(2,1)} %cot_in.1, bf16[512,384]{1,0:T(8,128)(2,1)} %tiles_in.1, s32[4,3]{1,0:T(4,128)} %src_in.1, bf16[8,128,128]{2,1,0:T(8,128)(2,1)} %bitcast.5, ...), custom_call_target="tpu_custom_call" | custom-call | tf_op jit(solution)/shard_map/layer/pallas_call | solution.py:646
  62.9 2.0 %store.1 = (bf16[512,128]{1,0:T(8,128)(2,1)}, bf16[512,128]{1,0:T(8,128)(2,1)}, f32[7,128,128]{2,1,0:T(8,128)}) custom-call(bf16[512,128]{1,0:T(8,128)(2,1)} %get-tuple-element.6.refs_0_, bf16[512,128]{1,0:T(8,128)(2,1)} %get-tuple-element.7.refs_1_, f32[7,128,128]{2,1,0:T(8,128)} %get-tuple-element.8.refs_2_), custom_call_target="tpu_custom_call" | custom-call | tf_op jit(solution)/shard_map/store/pallas_call | solution.py:673

commit v5 on v4

--- a/solution.py
+++ b/solution.py
@@ -28,7 +28,10 @@
 def dot_split(a, b, dims=NN):
     high = a.astype(BF16)
     low = (a - high.astype(F32)).astype(BF16)
-    return dot(high, b, dims) + dot(low, b, dims)
+    (left,), (right,) = dims
+    return dot(
+        jnp.concatenate([high, low], axis=left), jnp.concatenate([b, b], axis=right), dims
+    )
 
 
 def one_hot_rows(ids, first, count):
@@ -433,6 +436,9 @@
     t2 = t2.astype(BF16)
     counts = p1[:, C:][:, :k2]
     counts_t = counts.astype(F32).T.astype(BF16)
+    wide = p1[:, C:].astype(F32)
+    half = lax.broadcasted_iota(jnp.int32, (k1, C), 1) < k2
+    counts_twice = jnp.where(half, wide, pltpu.roll(wide, k2, 1)).astype(BF16)
 
     r_p2[q] = s_p2[b]
     arrived(7, r_p2.at[pl.ds(0, size_q - 1)])
@@ -455,7 +461,7 @@
     back2 = dot(sg2, up_ref[2], NT)
     back2_high = back2.astype(BF16)
     back2_low = (back2 - back2_high.astype(F32)).astype(BF16)
-    raw1 = raw1 + dot(counts, back2_high) + dot(counts, back2_low)
+    raw1 = raw1 + dot(counts_twice, jnp.concatenate([back2_high, back2_low], axis=0))
     sg1 = norm_back(raw1, normed1, inverse1).astype(BF16)
     raw0 = raw0 + dot_split(dot(group_bf[...], sg1), up_ref[1], NT)
     sg0 = norm_back(raw0, normed0, inverse0).astype(BF16)

time: 65.3 us -> 65.3 us (level)
  no operation moved by 1% of the time
where the time goes in v5:
time: 65.3 us; the launch traced here: 65.1 us
  Pallas kernels  64.3 us (98%)
  between operations  0.8 us (1%)
    pallas_call x1, Pallas kernels, on_device(): pl.pallas_call(functools.partial(kernel, size_x, size_y), out_shape=(jax....  62.3 us
    pallas_call x1, Pallas kernels, on_device(): pl.pallas_call(store, out_shape=tuple((jax.ShapeDtypeStruct(o.shape, o.dt...  2.01 us

profile of v5, /device:TPU:2, one launch (start us, length us, event | category | flops | bytes accessed | tf_op | source)
XLA Modules:
  0.0 65.1 jit_solution(3400817217068218576)
XLA Ops:
  0.6 62.3 %layer.1 = (bf16[512,128]{1,0:T(8,128)(2,1)}, bf16[512,128]{1,0:T(8,128)(2,1)}, f32[7,128,128]{2,1,0:T(8,128)}) custom-call(bf16[4,128,128]{2,1,0:T(8,128)(2,1)} %bitcast.6, bf16[512,128]{1,0:T(8,128)(2,1)} %cot_in.1, bf16[512,384]{1,0:T(8,128)(2,1)} %tiles_in.1, s32[4,3]{1,0:T(4,128)} %src_in.1, bf16[8,128,128]{2,1,0:T(8,128)(2,1)} %bitcast.5, ...), custom_call_target="tpu_custom_call" | custom-call | tf_op jit(solution)/shard_map/layer/pallas_call | solution.py:652
  63.0 2.0 %store.1 = (bf16[512,128]{1,0:T(8,128)(2,1)}, bf16[512,128]{1,0:T(8,128)(2,1)}, f32[7,128,128]{2,1,0:T(8,128)}) custom-call(bf16[512,128]{1,0:T(8,128)(2,1)} %get-tuple-element.6.refs_0_, bf16[512,128]{1,0:T(8,128)(2,1)} %get-tuple-element.7.refs_1_, f32[7,128,128]{2,1,0:T(8,128)} %get-tuple-element.8.refs_2_), custom_call_target="tpu_custom_call" | custom-call | tf_op jit(solution)/shard_map/store/pallas_call | solution.py:679

commit v6 on v5

--- a/solution.py
+++ b/solution.py
@@ -226,9 +226,11 @@
 
         lax.fori_loop(1, steps + 1, body, 0)
 
+    far_q = farthest["q"]
+    greet("q", size_q - far_q, far_q - 1)
+    greet("q", far_q - 1, 0)
     greet("z", reach, 0)
     greet("z", reach, size_z - reach - 1)
-    greet("q", size_q - 1, 0)
     beside = lax.rem(a + size_x - 1 + 2 * core, size_x)
     pl.semaphore_signal(barrier, inc=1, device_id=(beside, b), device_id_type=MESH)
 

time: 65.3 us -> 66 us (1.011)
  Pallas kernels: 64.3 us -> 65 us
    pallas_call x1, Pallas kernels: 62.3 us -> 63 us  [on_device(): pl.pallas_call(functools.partial(kernel, size_x, size_y), out_shape=(jax....]
where the time goes in v6:
time: 66 us; the launch traced here: 65.8 us
  Pallas kernels  65 us (98%)
  between operations  0.8 us (1%)
    pallas_call x1, Pallas kernels, on_device(): pl.pallas_call(functools.partial(kernel, size_x, size_y), out_shape=(jax....  63 us
    pallas_call x1, Pallas kernels, on_device(): pl.pallas_call(store, out_shape=tuple((jax.ShapeDtypeStruct(o.shape, o.dt...  2.01 us

profile of v6, /device:TPU:2, one launch (start us, length us, event | category | flops | bytes accessed | tf_op | source)
XLA Modules:
  0.0 65.8 jit_solution(7104647027244532939)
XLA Ops:
  0.6 63.0 %layer.1 = (bf16[512,128]{1,0:T(8,128)(2,1)}, bf16[512,128]{1,0:T(8,128)(2,1)}, f32[7,128,128]{2,1,0:T(8,128)}) custom-call(bf16[4,128,128]{2,1,0:T(8,128)(2,1)} %bitcast.6, bf16[512,128]{1,0:T(8,128)(2,1)} %cot_in.1, bf16[512,384]{1,0:T(8,128)(2,1)} %tiles_in.1, s32[4,3]{1,0:T(4,128)} %src_in.1, bf16[8,128,128]{2,1,0:T(8,128)(2,1)} %bitcast.5, ...), custom_call_target="tpu_custom_call" | custom-call | tf_op jit(solution)/shard_map/layer/pallas_call | solution.py:654
  63.6 2.0 %store.1 = (bf16[512,128]{1,0:T(8,128)(2,1)}, bf16[512,128]{1,0:T(8,128)(2,1)}, f32[7,128,128]{2,1,0:T(8,128)}) custom-call(bf16[512,128]{1,0:T(8,128)(2,1)} %get-tuple-element.6.refs_0_, bf16[512,128]{1,0:T(8,128)(2,1)} %get-tuple-element.7.refs_1_, f32[7,128,128]{2,1,0:T(8,128)} %get-tuple-element.8.refs_2_), custom_call_target="tpu_custom_call" | custom-call | tf_op jit(solution)/shard_map/store/pallas_call | solution.py:681
